TPU v7x, 512 devices: a whole 4x4x16 slice. The times are simulated.
512 devices in a mesh: group: 8 (over y, core), dev: 64 (over z, x).
Axes of the slice: x: 4, y: 4, z: 16, core: 2. Of those that a mesh axis runs over, the one named last changes fastest.
Arguments:
- level_set: bfloat16 [2048, 64, 64, 64], P(('group', 'dev')), may hold values from -6 to 6
- node_coords: float32 [3, 2048, 512], P(None, ('group', 'dev')), may hold values from -5 to 5
- position: float32 [3, 2048], P(None, ('group', 'dev')), may hold values from -2 to 2
- quaternion: float32 [4, 2048], P(None, ('group', 'dev')), may hold values from -1 to 1, as said below
- velocity: float32 [3, 2048], P(None, ('group', 'dev')), may hold values from -3 to 3
- spin: float32 [3, 2048], P(None, ('group', 'dev')), may hold values from -1.8 to 1.8
- mass: float32 [2048], P(('group', 'dev')), may hold values from 0.5 to 2
- grid_slot: int32 [65536], P(('group', 'dev')), may hold values from 0 to 3
- brick_anchor: int32 [3, 65536], P(None, ('group', 'dev')), may hold values from 27 to 29
- node_slot: int32 [65536], P(('group', 'dev')), may hold values from -1 to 3, as said below
- grid_cross: int32 [8192], P(('group', 'dev')), may hold values from 0 to 3
- anchor_cross: int32 [3, 8192], P(None, ('group', 'dev')), may hold values from 27 to 29
- node_cross: int32 [8192], P(('group', 'dev')), may hold values from -1 to 3, as said below
Outputs:
- new_position: float32 [3, 2048], P(None, ('group', 'dev'))
- new_quaternion: float32 [4, 2048], P(None, ('group', 'dev'))
- new_velocity: float32 [3, 2048], P(None, ('group', 'dev'))
- new_spin: float32 [3, 2048], P(None, ('group', 'dev'))
Inputs may be any that keep to these rules, and one draw needn't show every extreme that they name: Each column is a unit quaternion. `node_slot`: -1 marks a slot without a pair; the slot correspondence is the one of the step that defines pairs. `node_cross`: -1 marks a slot without a pair; every entry of the first group is -1.
All inputs are finite; a program needn't handle non-finite values.
Results may differ from a plain program's by a relative error of at most 0.0009.
Values may be sent and summed in bfloat16 or wider, within the bound.
A program may use at most 64 MiB of HBM per device.

v0:
```python
import jax
import jax.numpy as jnp
from jax import lax
from jax.sharding import PartitionSpec as P

GRID = 64
BRICK = 8


stiffness = 0.1
time_step = 0.5
spacing = 0.5
highest = lax.Precision.HIGHEST


def shifted(block, axis, distance):
    devices = range(lax.axis_size(axis))
    route = [(i - distance, i) for i in devices if i - distance in devices]
    return lax.ppermute(block, axis, route)


def rotation(quaternion):
    scalar_q = quaternion[0]
    vec_x = quaternion[1]
    vec_y = quaternion[2]
    vec_z = quaternion[3]
    first_row = jnp.stack(
        [
            1.0 - 2.0 * (vec_y * vec_y + vec_z * vec_z),
            2.0 * (vec_x * vec_y - scalar_q * vec_z),
            2.0 * (vec_x * vec_z + scalar_q * vec_y),
        ]
    )
    second_row = jnp.stack(
        [
            2.0 * (vec_x * vec_y + scalar_q * vec_z),
            1.0 - 2.0 * (vec_x * vec_x + vec_z * vec_z),
            2.0 * (vec_y * vec_z - scalar_q * vec_x),
        ]
    )
    third_row = jnp.stack(
        [
            2.0 * (vec_x * vec_z - scalar_q * vec_y),
            2.0 * (vec_y * vec_z + scalar_q * vec_x),
            1.0 - 2.0 * (vec_x * vec_x + vec_y * vec_y),
        ]
    )
    return jnp.stack([first_row, second_row, third_row])


def hat_weights(brick_coord):
    places = jnp.arange(BRICK).astype(jnp.float32)
    offsets = brick_coord[None, :] - places[:, None]
    center_hat = jnp.maximum(1.0 - jnp.abs(offsets), 0.0)
    upper_hat = jnp.maximum(1.0 - jnp.abs(offsets + spacing), 0.0)
    lower_hat = jnp.maximum(1.0 - jnp.abs(offsets - spacing), 0.0)
    return (center_hat, (upper_hat - lower_hat) / (2.0 * spacing))


def contact(node_arms, centre, brick_vals, anchor, place_j, turn_j):
    world_pos = centre[:, None] + node_arms
    relative = world_pos - place_j[:, None]
    in_frame = jnp.dot(turn_j.T, relative, precision=highest)
    brick_coord = in_frame + (GRID - 1) / 2.0 - anchor[:, None]
    hat_x, slope_x = hat_weights(brick_coord[0])
    hat_y, slope_y = hat_weights(brick_coord[1])
    hat_z, slope_z = hat_weights(brick_coord[2])
    contracted = jnp.einsum(
        "abc,kan->kbcn",
        brick_vals.astype(jnp.float32),
        jnp.stack([hat_x, slope_x]),
        precision=highest,
    )
    value_rows = jnp.sum(contracted[0] * hat_y[:, None, :], axis=0)
    along_y = jnp.sum(contracted[0] * slope_y[:, None, :], axis=0)
    along_x = jnp.sum(contracted[1] * hat_y[:, None, :], axis=0)
    level_value = jnp.sum(value_rows * hat_z, axis=0)
    gradient = jnp.stack(
        [
            jnp.sum(along_x * hat_z, axis=0),
            jnp.sum(along_y * hat_z, axis=0),
            jnp.sum(value_rows * slope_z, axis=0),
        ]
    )
    intersection = jnp.maximum(-level_value, 0.0)
    magnitude = jnp.sqrt(jnp.sum(gradient * gradient, axis=0))
    push_scale = stiffness * intersection / jnp.maximum(magnitude, 1.0)
    force_world = jnp.dot(turn_j, gradient * push_scale[None, :], precision=highest)
    net_force = jnp.sum(force_world, axis=1)
    twist_node = jnp.sum(jnp.cross(node_arms, force_world, axis=0), axis=1)
    twist_grid = -jnp.sum(jnp.cross(relative, force_world, axis=0), axis=1)
    return jnp.concatenate([net_force, twist_node, twist_grid])


def advance(position, quaternion, velocity, spin, mass, grain_loads):
    inertia = 0.4 * mass * (3.0 * GRID / 16.0) ** 2
    new_velocity = velocity + time_step * grain_loads[:3] / mass[None, :]
    new_spin = spin + time_step * grain_loads[3:] / inertia[None, :]
    new_position = position + time_step * new_velocity
    turning_scalar = -jnp.sum(new_spin * quaternion[1:], axis=0)
    turning_vector = quaternion[0][None, :] * new_spin + jnp.cross(new_spin, quaternion[1:], axis=0)
    unnormal = quaternion + 0.5 * time_step * jnp.concatenate(
        [turning_scalar[None, :], turning_vector]
    )
    new_quaternion = unnormal / jnp.sqrt(jnp.sum(unnormal * unnormal, axis=0))[None, :]
    return (new_position, new_quaternion, new_velocity, new_spin)


def contacts_blocked(node_arms, centres, bricks, anchors, places, rotations_j):
    per_block = 16
    blocks = node_arms.shape[0] // per_block

    def regroup(array):
        return array.reshape((blocks, per_block) + array.shape[1:])

    def run_block(pair_data):
        return jax.vmap(contact)(
            pair_data[0], pair_data[1], pair_data[2], pair_data[3], pair_data[4], pair_data[5]
        )

    grouped = jax.tree.map(regroup, (node_arms, centres, bricks, anchors, places, rotations_j))
    return lax.map(run_block, grouped).reshape(-1, 9)


def cut_bricks(level_set, grain_index, corners):
    grains = level_set.shape[0]
    grid_len = level_set.shape[1]
    base = grid_len // 2 - 5
    span = BRICK + 2
    window = level_set[:, base : base + span, base : base + span, base : base + span].astype(
        jnp.float32
    )
    places = jnp.arange(span, dtype=jnp.int32)
    offsets = jnp.arange(BRICK, dtype=jnp.int32)

    def selector(corner_dim):
        return (
            places[None, None, :] == (corner_dim - base)[:, None, None] + offsets[None, :, None]
        ).astype(jnp.float32)

    pick = (grain_index[:, None] == jnp.arange(grains, dtype=jnp.int32)[None, :]).astype(
        jnp.float32
    )
    select_x = selector(corners[:, 0])
    select_y = selector(corners[:, 1])
    select_z = selector(corners[:, 2])
    count = grain_index.shape[0]
    combined = (pick[:, None, :, None] * select_x[:, :, None, :]).reshape(
        count * BRICK, grains * span
    )
    first = jnp.dot(
        combined, window.reshape(grains * span, span * span), precision=highest
    ).reshape(count, BRICK, span, span)
    second = jnp.einsum("sajk,sbj->sabk", first, select_y, precision=highest)
    third = jnp.einsum("sabk,sck->sabc", second, select_z, precision=highest)
    return third.astype(jnp.bfloat16)


def body(
    level_set,
    node_coords,
    position,
    quaternion,
    velocity,
    spin,
    mass,
    grid_slot,
    brick_anchor,
    node_slot,
    grid_cross,
    anchor_cross,
    node_cross,
):
    grains = level_set.shape[0]
    dev_count = lax.axis_size("dev")
    slot_count = grid_slot.shape[0]
    per_peer = slot_count // dev_count
    rotations = rotation(quaternion)
    arms_all = jnp.einsum("klg,lgn->gkn", rotations, node_coords, precision=highest)
    grain_ids = jnp.arange(grains, dtype=jnp.int32)
    pick_node = (node_slot[:, None] == grain_ids[None, :]).astype(jnp.float32)
    pick_cross_node = (node_cross[:, None] == grain_ids[None, :]).astype(jnp.float32)
    pick_grid = (grid_slot[:, None] == grain_ids[None, :]).astype(jnp.float32)
    pick_cross_grid = (grid_cross[:, None] == grain_ids[None, :]).astype(jnp.float32)

    def node_side(picks):
        return (
            jnp.einsum("sg,gkn->skn", picks, arms_all, precision=highest),
            jnp.dot(picks, position.T, precision=highest),
            jnp.sum(picks, axis=1),
        )

    def grid_side(picks):
        return (
            jnp.dot(picks, position.T, precision=highest),
            jnp.einsum("sg,klg->skl", picks, rotations, precision=highest),
        )

    slot_arms, slot_centres, slot_valid = node_side(pick_node)
    cross_arms_own, cross_centres, cross_valid = node_side(pick_cross_node)
    grid_places, grid_rotations = grid_side(pick_grid)
    cross_places, cross_rotations = grid_side(pick_cross_grid)
    slot_bricks = cut_bricks(level_set, grid_slot, brick_anchor.T)
    cross_bricks_own = cut_bricks(level_set, grid_cross, anchor_cross.T)
    slot_corner = brick_anchor.T.astype(jnp.float32)
    cross_corner = anchor_cross.T.astype(jnp.float32)
    got_arms, got_centres, got_valid = (
        lax.all_to_all(
            slot_arms.reshape(dev_count, per_peer, 3, -1),
            "dev",
            split_axis=0,
            concat_axis=0,
            tiled=True,
        ),
        lax.all_to_all(
            slot_centres.reshape(dev_count, per_peer, 3),
            "dev",
            split_axis=0,
            concat_axis=0,
            tiled=True,
        ),
        lax.all_to_all(
            slot_valid.reshape(dev_count, per_peer), "dev", split_axis=0, concat_axis=0, tiled=True
        ),
    )
    up_arms, up_centres, up_valid = shifted(
        (cross_arms_own, cross_centres, cross_valid), "group", -1
    )
    arms_in = jnp.concatenate([got_arms.reshape(slot_count, 3, -1), up_arms], axis=0)
    centres_in = jnp.concatenate([got_centres.reshape(slot_count, 3), up_centres], axis=0)
    valid_in = jnp.concatenate([got_valid.reshape(slot_count), up_valid], axis=0)
    bricks_in = jnp.concatenate([slot_bricks, cross_bricks_own], axis=0)
    corners_in = jnp.concatenate([slot_corner, cross_corner], axis=0)
    places_in = jnp.concatenate([grid_places, cross_places], axis=0)
    rotations_in = jnp.concatenate([grid_rotations, cross_rotations], axis=0)
    pair_loads = (
        contacts_blocked(arms_in, centres_in, bricks_in, corners_in, places_in, rotations_in)
        * valid_in[:, None]
    )
    grid_load = jnp.concatenate([-pair_loads[:, :3], pair_loads[:, 6:]], axis=1)
    own_grid = jnp.dot(pick_grid.T, grid_load[:slot_count], precision=highest) + jnp.dot(
        pick_cross_grid.T, grid_load[slot_count:], precision=highest
    )
    returned = lax.all_to_all(
        pair_loads[:slot_count, :6].reshape(dev_count, per_peer, 6),
        "dev",
        split_axis=0,
        concat_axis=0,
        tiled=True,
    ).reshape(slot_count, 6)
    from_below = shifted(pair_loads[slot_count:, :6], "group", 1)
    own_node = jnp.dot(pick_node.T, returned, precision=highest) + jnp.dot(
        pick_cross_node.T, from_below, precision=highest
    )
    totals = own_node + own_grid
    new_position, new_quaternion, new_velocity, new_spin = advance(
        position, quaternion, velocity, spin, mass, totals.T
    )
    return (new_position, new_quaternion, new_velocity, new_spin)


def solution(mesh):
    in_specs = (
        P(("group", "dev"), None, None, None),
        P(None, ("group", "dev"), None),
        P(None, ("group", "dev")),
        P(None, ("group", "dev")),
        P(None, ("group", "dev")),
        P(None, ("group", "dev")),
        P(("group", "dev")),
        P(("group", "dev")),
        P(None, ("group", "dev")),
        P(("group", "dev")),
        P(("group", "dev")),
        P(None, ("group", "dev")),
        P(("group", "dev")),
    )
    out_specs = (
        P(None, ("group", "dev")),
        P(None, ("group", "dev")),
        P(None, ("group", "dev")),
        P(None, ("group", "dev")),
    )
    return jax.shard_map(body, mesh=mesh, in_specs=in_specs, out_specs=out_specs, check_vma=False)
```

profile of v0, /device:TPU:24, one launch (start us, length us, event | category | flops | bytes accessed | tf_op | source)
XLA Modules:
  0.0 248.3 jit_solution(6178279794497910959)
XLA Ops:
  3.2 1.5 fusion.90
  4.7 2.1 collective-permute-start.1
  6.8 1.4 fusion.100
  8.2 2.6 %collective-permute-start = (f32[16,3]{0,1:T(4,128)}, f32[16,3]{0,1:T(4,128)}, u32[]{:S(2)}, u32[]{:S(2)}) collective-permute-start(f32[16,3]{0,1:T(4,128)} %fusion.100), channel_id=1, source_target_pairs={{64,0},{128,64},{192,128},{256,192},{320,256},{384,320},{448,384},... | collective-permute-start | bytes 584 | tf_op jit(solution)/shard_map/ppermute | solution.py:19
  12.2 18.6 %all-to-all-start.2 = ((f32[64,1,2]{2,1,0:T(1,128)}), f32[64,1,2]{2,1,0:T(1,128)S(1)}, u32[]{:S(2)}, u32[]{:S(2)}) async-start(f32[64,1,2]{2,1,0:T(1,128)} %bitcast.62), calls=%async_computation.2 | async-start | bytes 65536 | tf_op jit(solution)/shard_map/all_to_all | solution.py:222
  32.0 1.9 collective-permute-start.2
  36.6 1.6 fusion.103
  41.6 7.6 %copy.131 = f32[128,8,10,10]{3,2,1,0:T(8,128)} copy(f32[128,8,10,10]{0,3,2,1:T(8,128)S(1)} %fusion.78) | data formatting | bytes 819200 | tf_op jit(solution)/shard_map/dot_general | solution.py:151
  49.3 5.7 %fusion.70 = f32[128,8,8,10]{3,1,2,0:T(8,128)S(1)} fusion(f32[128,8,10,10]{3,2,1,0:T(8,128)} %copy.131, s32[128,8]{1,0:T(8,128)S(1)} %get-tuple-element.251), kind=kOutput, calls=%fused_computation.115 | convolution fusion | flops 9840640 | bytes 741376 | tf_op jit(solution)/shard_map/sajk,sbj->sabk/dot_general | solution.py:154
  55.0 2.4 fusion.64
  57.5 15.1 %all-to-all-start = ((f32[64,2,3]{2,1,0:T(2,128)}), f32[64,2,3]{2,1,0:T(2,128)S(1)}, u32[]{:S(2)}, u32[]{:S(2)}) async-start(f32[64,2,3]{2,1,0:T(2,128)} %bitcast.32), calls=%async_computation | async-start | bytes 131072 | tf_op jit(solution)/shard_map/all_to_all | solution.py:215
  74.2 2.3 copy.126
  77.4 2.1 copy.134
  79.5 9.3 %all-to-all-done = f32[64,2,3]{2,1,0:T(2,128)S(1)} async-done(((f32[64,2,3]{2,1,0:T(2,128)}), f32[64,2,3]{2,1,0:T(2,128)S(1)}, u32[]{:S(2)}, u32[]{:S(2)}) %all-to-all-start) | async-done | bytes 1568 | tf_op jit(solution)/shard_map/all_to_all | solution.py:215
  88.8 6.0 %all-to-all-start.1 = ((f32[64,2,3,512]{3,1,2,0:T(2,128)}), f32[64,2,3,512]{3,1,2,0:T(2,128)S(1)}, u32[]{:S(2)}, u32[]{:S(2)}) async-start(f32[64,2,3,512]{3,1,2,0:T(2,128)} %copy.126), calls=%async_computation.1 | async-start | bytes 1572864 | tf_op jit(solution)/shard_map/all_to_all | solution.py:208
  97.1 3.8 %copy.174 = bf16[144,8,8,8]{1,3,2,0:T(8,128)(2,1)S(1)} copy(bf16[144,8,8,8]{0,3,2,1:T(8,128)(2,1)S(1)} %pad_maximum_fusion.3) | data formatting | bytes 294912 | tf_op jit(solution)/shard_map/while | solution.py:122
  107.1 32.1 %all-to-all-done.1 = f32[64,2,3,512]{3,1,2,0:T(2,128)S(1)} async-done(((f32[64,2,3,512]{3,1,2,0:T(2,128)}), f32[64,2,3,512]{3,1,2,0:T(2,128)S(1)}, u32[]{:S(2)}, u32[]{:S(2)}) %all-to-all-start.1) | async-done | bytes 786464 | tf_op jit(solution)/shard_map/all_to_all | solution.py:208
  140.4 1.7 reshape.678
  142.1 1.9 pad_maximum_fusion.2
  144.0 78.5 %while.13 = (s32[]{:T(128)}, f32[9,16,9]{2,1,0:T(8,128)S(1)}, f32[9,16,3,3]{2,3,1,0:T(4,128)}, f32[9,16,3]{1,0,2:T(8,128)S(1)}, f32[9,16,3,512]{3,1,0,2:T(8,128)...) while((s32[]{:T(128)}, f32[9,16,9]{2,1,0:T(8,128)S(1)}, ...), condition=%wide.region_12.14_spmd, body=%wide.region_0.13_spmd.sunk | while | flops 109232328 | bytes 15276529 | solution.py:122
  146.7 1.8 convolution_bitcast_fusion.3
  155.4 1.8 convolution_bitcast_fusion.3
  164.1 1.8 convolution_bitcast_fusion.3
  172.9 1.8 convolution_bitcast_fusion.3
  181.6 1.8 convolution_bitcast_fusion.3
  190.3 1.8 convolution_bitcast_fusion.3
  199.0 1.8 convolution_bitcast_fusion.3
  207.7 1.8 convolution_bitcast_fusion.3
  216.4 1.8 convolution_bitcast_fusion.3
  223.3 5.8 %all-to-all-start.3 = ((f32[64,2,6]{2,1,0:T(2,128)}), f32[64,2,6]{2,1,0:T(2,128)S(1)}, u32[]{:S(2)}, u32[]{:S(2)}) async-start(f32[64,2,6]{2,1,0:T(2,128)} %bitcast.63), calls=%async_computation.3 | async-start | bytes 131072 | tf_op jit(solution)/shard_map/all_to_all | solution.py:244
  229.2 1.9 collective-permute-start.3
  231.2 13.2 %all-to-all-done.3 = f32[64,2,6]{2,1,0:T(2,128)S(1)} async-done(((f32[64,2,6]{2,1,0:T(2,128)}), f32[64,2,6]{2,1,0:T(2,128)S(1)}, u32[]{:S(2)}, u32[]{:S(2)}) %all-to-all-start.3) | async-done | bytes 3104 | tf_op jit(solution)/shard_map/all_to_all | solution.py:244
  (410 shorter events, 89.1 us)
Async XLA Ops:
  0.6 2.4 copy-start
  4.7 137.4 %collective-permute-start.1 = (f32[16,3,512]{2,0,1:T(8,128)}, f32[16,3,512]{2,0,1:T(8,128)}, u32[]{:S(2)}, u32[]{:S(2)}) collective-permute-start(f32[16,3,512]{2,0,1:T(8,128)} %fusion.90), channel_id=1, source_target_pairs={{64,0},{128,64},{192,128},{256,192},{320,256},{384,320},{448,384},... | collective-permute-start | bytes 294920 | tf_op jit(solution)/shard_map/ppermute | solution.py:19
  8.2 98.1 %collective-permute-start = (f32[16,3]{0,1:T(4,128)}, f32[16,3]{0,1:T(4,128)}, u32[]{:S(2)}, u32[]{:S(2)}) collective-permute-start(f32[16,3]{0,1:T(4,128)} %fusion.100), channel_id=1, source_target_pairs={{64,0},{128,64},{192,128},{256,192},{320,256},{384,320},{448,384},... | collective-permute-start | bytes 584 | tf_op jit(solution)/shard_map/ppermute | solution.py:19
  12.2 45.3 %all-to-all-start.2 = ((f32[64,1,2]{2,1,0:T(1,128)}), f32[64,1,2]{2,1,0:T(1,128)S(1)}, u32[]{:S(2)}, u32[]{:S(2)}) async-start(f32[64,1,2]{2,1,0:T(1,128)} %bitcast.62), calls=%async_computation.2 | async-start | bytes 65536 | tf_op jit(solution)/shard_map/all_to_all | solution.py:222
  32.0 73.7 %collective-permute-start.2 = (f32[16]{0:T(128)}, f32[16]{0:T(128)}, u32[]{:S(2)}, u32[]{:S(2)}) collective-permute-start(f32[16]{0:T(128)} %convert_reduce_fusion), channel_id=1, source_target_pairs={{64,0},{128,64},{192,128},{256,192},{320,256},{384,320},{448,384},... | collective-permute-start | bytes 200 | tf_op jit(solution)/shard_map/ppermute | solution.py:19
  41.6 7.6 %copy-start.4 = (s32[3,16]{1,0:T(4,128)S(1)}, s32[3,16]{1,0:T(4,128)}, u32[]{:S(2)}) copy-start(s32[3,16]{1,0:T(4,128)} %param.28) | copy-start | bytes 580
  55.0 17.7 %copy-start.3 = (f32[4,4]{1,0:T(4,128)S(1)}, f32[4,4]{1,0:T(4,128)}, u32[]{:S(2)}) copy-start(f32[4,4]{1,0:T(4,128)} %param.20) | copy-start | bytes 196
  55.0 17.8 %copy-start.2 = (f32[3,4]{1,0:T(4,128)S(1)}, f32[3,4]{1,0:T(4,128)}, u32[]{:S(2)}) copy-start(f32[3,4]{1,0:T(4,128)} %param.19) | copy-start | bytes 148
  57.4 37.4 %copy-start.8 = (s32[16]{0:T(128)S(1)}, s32[16]{0:T(128)}, u32[]{:S(2)}) copy-start(s32[16]{0:T(128)} %param.27) | copy-start | bytes 196
  57.5 31.2 %all-to-all-start = ((f32[64,2,3]{2,1,0:T(2,128)}), f32[64,2,3]{2,1,0:T(2,128)S(1)}, u32[]{:S(2)}, u32[]{:S(2)}) async-start(f32[64,2,3]{2,1,0:T(2,128)} %bitcast.32), calls=%async_computation | async-start | bytes 131072 | tf_op jit(solution)/shard_map/all_to_all | solution.py:215
  79.5 22.3 %copy-start.7 = (s32[128]{0:T(128)S(1)}, s32[128]{0:T(128)}, u32[]{:S(2)}) copy-start(s32[128]{0:T(128)} %param.24) | copy-start | bytes 1540
  79.5 22.5 %copy-start.5 = (s32[3,128]{1,0:T(4,128)S(1)}, s32[3,128]{1,0:T(4,128)}, u32[]{:S(2)}) copy-start(s32[3,128]{1,0:T(4,128)} %param.25) | copy-start | bytes 4612
  88.8 50.5 %all-to-all-start.1 = ((f32[64,2,3,512]{3,1,2,0:T(2,128)}), f32[64,2,3,512]{3,1,2,0:T(2,128)S(1)}, u32[]{:S(2)}, u32[]{:S(2)}) async-start(f32[64,2,3,512]{3,1,2,0:T(2,128)} %copy.126), calls=%async_computation.1 | async-start | bytes 1572864 | tf_op jit(solution)/shard_map/all_to_all | solution.py:208
  100.9 43.1 %copy-start.1 = (f32[9,16,9]{2,1,0:T(8,128)S(1)}, f32[9,16,9]{2,1,0:T(8,128)}, u32[]{:S(2)}) copy-start(f32[9,16,9]{2,1,0:T(8,128)} %custom-call) | copy-start | bytes 15556
  144.0 100.4 %copy-start.10 = (s32[128]{0:T(128)S(1)}, s32[128]{0:T(128)}, u32[]{:S(2)}) copy-start(s32[128]{0:T(128)} %param.26) | copy-start | bytes 1540
  144.0 100.6 %copy-start.6 = (s32[16]{0:T(128)S(1)}, s32[16]{0:T(128)}, u32[]{:S(2)}) copy-start(s32[16]{0:T(128)} %param.29) | copy-start | bytes 196
  144.0 100.7 %copy-start.9 = (s32[16]{0:T(128)S(1)}, s32[16]{0:T(128)}, u32[]{:S(2)}) copy-start(s32[16]{0:T(128)} %param.27) | copy-start | bytes 196
  144.0 100.8 %copy-start.12 = (f32[4]{0:T(128)S(1)}, f32[4]{0:T(128)}, u32[]{:S(2)}) copy-start(f32[4]{0:T(128)} %param.23) | copy-start | bytes 52
  144.0 101.9 %copy-start.11 = (f32[4]{0:T(128)S(1)}, f32[4]{0:T(128)}, u32[]{:S(2)}) copy-start(f32[4]{0:T(128)} %get-tuple-element.227) | copy-start | bytes 52
  223.3 21.1 %all-to-all-start.3 = ((f32[64,2,6]{2,1,0:T(2,128)}), f32[64,2,6]{2,1,0:T(2,128)S(1)}, u32[]{:S(2)}, u32[]{:S(2)}) async-start(f32[64,2,6]{2,1,0:T(2,128)} %bitcast.63), calls=%async_computation.3 | async-start | bytes 131072 | tf_op jit(solution)/shard_map/all_to_all | solution.py:244
  229.2 15.4 %collective-permute-start.3 = (f32[16,6]{0,1:T(8,128)S(1)}, f32[16,6]{0,1:T(8,128)S(1)}, u32[]{:S(2)}, u32[]{:S(2)}) collective-permute-start(f32[16,6]{0,1:T(8,128)S(1)} %slice.200), channel_id=1, source_target_pairs={{0,64},{64,128},{128,192},{192,256},{256,320},{320,384},{384,448},... | collective-permute-start | bytes 1160 | tf_op jit(solution)/shard_map/ppermute | solution.py:19
where the time goes:
time: 251 us; the launch traced here: 248 us
  matrix products  57.9 us (23%)
  waiting for transfers between devices  54.6 us (22%)
  starting transfers between devices  54 us (22%)
  local copies, waits for them, and re-layouts  42.4 us (17%)
  other arithmetic  36.9 us (15%)
    all_to_all x1, waiting for transfers between devices, body(): lax.all_to_all(slot_arms.reshape(dev_count, per_peer, 3, -1), 'dev', spli...  32.1 us
    all_to_all x1, starting transfers between devices, body(): lax.all_to_all(slot_valid.reshape(dev_count, per_peer), 'dev', split_axis...  18.6 us
    dot_general x9, matrix products, contact(): jnp.einsum('abc,kan->kbcn', brick_vals.astype(jnp.float32), jnp.stack([ha...  16.1 us
    all_to_all x1, starting transfers between devices, body(): lax.all_to_all(slot_centres.reshape(dev_count, per_peer, 3), 'dev', split...  15.1 us
    all_to_all x1, waiting for transfers between devices, body(): lax.all_to_all(pair_loads[:slot_count, :6].reshape(dev_count, per_peer, 6...  13.2 us
    dot_general x9, matrix products, contact(): jnp.dot(turn_j, gradient * push_scale[None, :], precision=highest)  11.8 us
    dot_general x9, matrix products, contact(): in_frame = jnp.dot(turn_j.T, relative, precision=highest)  10.6 us
    all_to_all x1, waiting for transfers between devices, body(): lax.all_to_all(slot_centres.reshape(dev_count, per_peer, 3), 'dev', split...  9.28 us
  transfers between devices with their start and end apart: 8, of which 3 were waited for; matrix products, arithmetic and copies ran while one was open for 20% of the time, Pallas kernels for 0%

commit v1 on v0

v1 whole, which is shorter than its diff:
```python
import jax
import jax.numpy as jnp
import numpy as np
from jax import lax
from jax.experimental import pallas as pl
from jax.experimental.pallas import tpu as pltpu
from jax.sharding import PartitionSpec as P

MESH = pl.DeviceIdType.MESH
f32, bf16, i32 = jnp.float32, jnp.bfloat16, jnp.int32

GRID = 64
GROUPS = 8
DEVS = 64
GRAINS = 4
NODES = 512
BASE = GRID // 2 - 5
SPAN = 10
TILES = DEVS + 8
PAIRS = 2 * TILES
LEVELS = 32766.0
stiffness = 0.1
time_step = 0.5
R_PART = (0, 0, 1, 1, 0, 2)
P_PART = (0, 1, 0, 1, 2, 0)


def spread_matrix():
    spread = np.zeros((3 * 128, 3 * 128), np.float32)
    for k in range(3):
        for combo, part in enumerate(R_PART):
            for m in range(3):
                for grain in range(GRAINS):
                    spread[128 * part + 3 * m + k, 128 * k + 16 * combo + 4 * m + grain] = 1.0
            spread[128 * part + 9 + k, 128 * k + 16 * combo + 12] = 1.0
    return spread


def iota(shape, dim):
    return lax.broadcasted_iota(i32, shape, dim)


def parts(x):
    first = x.astype(bf16)
    rest = x - first.astype(f32)
    second = rest.astype(bf16)
    third = (rest - second.astype(f32)).astype(bf16)
    return first, second, third


def matmul(a, b):
    return jnp.dot(a, b, preferred_element_type=f32)


def matmul_nt(a, b):
    return lax.dot_general(a, b, (((1,), (1,)), ((), ())), preferred_element_type=f32)


def hat(t):
    return jnp.maximum(1.0 - jnp.abs(t), 0.0)


def slope(t):
    return jnp.maximum(jnp.minimum(-2.0 * t, jnp.maximum(t + 1.5, 0.0)), jnp.minimum(t - 1.5, 0.0))


def take(table, index):
    return jnp.take_along_axis(table, index, axis=1, mode="promise_in_bounds")


def near(u):
    r = jnp.floor(u + 0.5)
    f = u - r
    e = jnp.abs(f)
    up = f >= 0.0
    half = jnp.where(up, 0.5, -0.5)
    step = jnp.where(up, 1, -1)
    a = r.astype(i32)
    b = a + step
    c = a - step
    in_a, in_b, in_c = ((i & -8) == 0 for i in (a, b, c))
    hats = (jnp.where(in_a, 1.0 - e, 0.0), jnp.where(in_b, e, 0.0))
    slopes = (
        jnp.where(in_a, -2.0 * f, 0.0),
        jnp.where(in_b, f + half, 0.0),
        jnp.where(in_c, f - half, 0.0),
    )
    return (a & 7, b & 7, c & 7), hats, slopes


def contact(even, odd, scale, u):
    rx = jnp.floor(u[0] + 0.5).astype(i32)
    bit_e = ((rx + 1) << 4) & 64
    bit_o = ((rx - 1) << 4) & 64
    de = u[0] - (bit_e >> 4).astype(f32)
    do = u[0] - (bit_o >> 4).astype(f32) - 2.0
    tiny = 1.0 / 65536.0

    def lanes(weight):
        hi_e, hi_o = weight(de - 1.0) * tiny, weight(do - 1.0) * tiny
        return weight(de) - hi_e, hi_e, weight(do) - hi_o, hi_o

    hx, sx = lanes(hat), lanes(slope)
    yi, hy, sy = near(u[1])
    zi, hz, sz = near(u[2])
    yi = [i << 3 for i in yi]

    def column(j, k, with_slope):
        place = yi[j] | zi[k]
        we, wo = take(even, bit_e | place), take(odd, bit_o | place)
        values = (((we << 16) >> 16).astype(f32), we.astype(f32), ((wo << 16) >> 16).astype(f32), wo.astype(f32))

        def meet(w):
            return (values[0] * w[0] + values[1] * w[1]) + (values[2] * w[2] + values[3] * w[3])

        return meet(hx), (meet(sx) if with_slope else None)

    rows, rows_x, rows_z = [], [], []
    for j in range(2):
        v0, s0 = column(j, 0, True)
        v1, s1 = column(j, 1, True)
        v2, _ = column(j, 2, False)
        rows.append(v0 * hz[0] + v1 * hz[1])
        rows_x.append(s0 * hz[0] + s1 * hz[1])
        rows_z.append(v0 * sz[0] + v1 * sz[1] + v2 * sz[2])
    v0, _ = column(2, 0, False)
    v1, _ = column(2, 1, False)
    rows.append(v0 * hz[0] + v1 * hz[1])
    phi = (rows[0] * hy[0] + rows[1] * hy[1]) * scale
    gx = (rows_x[0] * hy[0] + rows_x[1] * hy[1]) * scale
    gy = (rows[0] * sy[0] + rows[1] * sy[1] + rows[2] * sy[2]) * scale
    gz = (rows_z[0] * hy[0] + rows_z[1] * hy[1]) * scale
    push = stiffness * jnp.maximum(-phi, 0.0) * lax.rsqrt(jnp.maximum(gx * gx + gy * gy + gz * gz, 1.0))
    g = (gx * push, gy * push, gz * push)
    return g + cross(u, g)


def cross(a, b):
    return (a[1] * b[2] - a[2] * b[1], a[2] * b[0] - a[0] * b[2], a[0] * b[1] - a[1] * b[0])


def kernel(
    level_ref, coords_ref, position_ref, quaternion_ref, velocity_ref, spin_ref, mass_ref, grid_ref, anchor_ref, node_ref,
    grid_cross_ref, anchor_cross_ref, node_cross_ref, spread_ref,
    new_position_ref, new_quaternion_ref, new_velocity_ref, new_spin_ref,
    window, attr, cols, slab, pose, points, out_msg, in_msg, metas, sums, out_ret, in_ret, back,
    window_sem, send_sem, recv_sem, ret_send_sem, ret_recv_sem, cross_sem,
):
    g = lax.axis_index("group")
    d = lax.axis_index("dev")
    up, down = lax.rem(g + 1, GROUPS), lax.rem(g + GROUPS - 1, GROUPS)
    barrier = pltpu.get_barrier_semaphore()

    def greet(k, _):
        e = lax.rem(d + k, DEVS)
        pl.semaphore_signal(barrier, inc=1, device_id=(g, e), device_id_type=MESH)
        return 0

    load = pltpu.make_async_copy(
        level_ref.at[:, BASE : BASE + SPAN, 16:48, :], window, window_sem
    )
    load.start()
    lax.fori_loop(1, DEVS, greet, 0)
    for other in (up, down):
        pl.semaphore_signal(barrier, inc=1, device_id=(other, d), device_id_type=MESH)

    attr[...] = jnp.zeros_like(attr)
    attr[0:1, 0:128] = (grid_ref[...] + 1).astype(f32)
    attr[0:1, 128:144] = (grid_cross_ref[...] + 1).astype(f32)
    attr[1:4, 0:128] = (anchor_ref[...] - BASE).astype(f32)
    attr[1:4, 128:144] = (anchor_cross_ref[...] - BASE).astype(f32)
    attr[4:5, 0:128] = (node_ref[...] + 1).astype(f32)
    attr[4:5, 128:144] = (node_cross_ref[...] + 1).astype(f32)
    slot_to = iota((256, 256), 0)
    order = (iota((256, 256), 1) == ((slot_to & 127) << 1) + (slot_to >> 7)).astype(f32).astype(bf16)
    attr_b = attr[...].astype(bf16)
    attr_rows = matmul_nt(attr_b, order)
    cols[...] = matmul_nt(order, attr_b)

    w, x, y, z = (quaternion_ref[k : k + 1, :] for k in range(4))
    rot = (
        1.0 - 2.0 * (y * y + z * z), 2.0 * (x * y - w * z), 2.0 * (x * z + w * y),
        2.0 * (x * y + w * z), 1.0 - 2.0 * (x * x + z * z), 2.0 * (y * z - w * x),
        2.0 * (x * z - w * y), 2.0 * (y * z + w * x), 1.0 - 2.0 * (x * x + y * y),
    )
    pos = [position_ref[m : m + 1, :] for m in range(3)]
    pose[...] = jnp.zeros_like(pose)
    for n in range(9):
        pose[n : n + 1, 0:GRAINS] = rot[n]
    for k in range(3):
        turned = rot[k] * pos[0] + rot[3 + k] * pos[1] + rot[6 + k] * pos[2]
        pose[9 + k : 10 + k, 0:GRAINS] = ((GRID - 1) / 2.0 - BASE) - turned
        pose[16 + k : 17 + k, 0:GRAINS] = pos[k]
    pose_cols = pose[...].T

    points[...] = jnp.zeros_like(points)
    world = []
    for m in range(3):
        p = pose_cols[0:GRAINS, 16 + m : 17 + m]
        for n in range(3):
            p = p + pose_cols[0:GRAINS, 3 * m + n : 3 * m + n + 1] * coords_ref[n]
        world.append(p)
    ones = jnp.where(iota((GRAINS, NODES), 0) == 0, 1.0, 0.0)
    world = parts(jnp.concatenate(world + [ones], axis=0))
    for combo, part in enumerate(P_PART):
        points[16 * combo : 16 * combo + 16, :] = world[part]

    lane64 = iota((64, 384), 1)
    select_z = (iota((64, 384), 0) == BASE + (lane64 >> 7) + (lane64 & 7)).astype(f32).astype(bf16)
    place_y = iota((16, 128), 0)
    lane_y = (iota((16, 128), 1) >> 3) & 7
    load.wait()
    planes = matmul(window[...].reshape(GRAINS * SPAN * 32, GRID), select_z)
    planes = planes.reshape(GRAINS * SPAN, 32, 384)[:, 8:24, :]
    low_half = iota((40, 128), 1) < 64
    for ay in range(3):
        keep = (place_y == BASE - 24 + ay + lane_y).astype(f32)
        for az in range(3):
            picked = jnp.sum(planes[:, :, 128 * az : 128 * az + 128] * keep[None], axis=1)
            q = 3 * ay + az
            slab[40 * q : 40 * q + 40, :] = jnp.where(low_half, picked, pltpu.roll(picked, 36, 0))
    slab[360:384, :] = jnp.zeros((24, 128), f32)
    code = [
        (cols[128 * c : 128 * c + TILES, 2:3] * 3.0 + cols[128 * c : 128 * c + TILES, 3:4]) * 40.0
        + (cols[128 * c : 128 * c + TILES, 0:1] - 1.0) * 10.0
        + cols[128 * c : 128 * c + TILES, 1:2]
        for c in range(2)
    ]
    code = jnp.concatenate([code[c] + float(j) for c in range(2) for j in range(4)], axis=0).astype(i32)
    pick = (iota((8 * TILES, 384), 1) == code).astype(f32).astype(bf16)
    bricks = matmul(pick, slab[...].astype(bf16))
    lane = iota((TILES, 128), 1)
    pose_parts = parts(pose_cols)
    unit = jnp.where(lane < 9, 2.0**30, jnp.where(lane < 12, 2.0**27, 2.0**28))
    for c in range(2):
        rows = [bricks[TILES * (4 * c + j) : TILES * (4 * c + j + 1), :] for j in range(4)]
        most = jnp.maximum(
            jnp.maximum(jnp.abs(rows[0]), jnp.abs(rows[1])), jnp.maximum(jnp.abs(rows[2]), jnp.abs(rows[3]))
        )
        most = jnp.maximum(jnp.max(most, axis=1, keepdims=True), 1e-6)
        inverse = LEVELS / most
        level = [jnp.floor(row * inverse + 0.5).astype(i32) for row in rows]
        out_msg[pl.ds(3 * c, TILES, stride=8), :] = (level[1] << 16) + level[0]
        out_msg[pl.ds(3 * c + 1, TILES, stride=8), :] = (level[3] << 16) + level[2]
        own = cols[128 * c : 128 * c + TILES, :]
        grain = (own[:, 0:1].astype(i32) - 1 == lane).astype(f32).astype(bf16)
        meta = matmul(grain, pose_parts[0]) + matmul(grain, pose_parts[1]) + matmul(grain, pose_parts[2])
        for k in range(3):
            meta = meta - jnp.where(lane == 9 + k, own[:, 1 + k : 2 + k], 0.0)
        meta = jnp.where(lane == 12, most, jnp.where(lane < 12, meta, 0.0))
        out_msg[pl.ds(3 * c + 2, TILES, stride=8), :] = (meta * unit).astype(i32)

    def message(e, other):
        return pltpu.make_async_remote_copy(
            src_ref=out_msg.at[pl.ds(pl.multiple_of(8 * e, 8), ROWS)],
            dst_ref=in_msg.at[pl.ds(pl.multiple_of(8 * other, 8), ROWS)],
            send_sem=send_sem.at[e],
            recv_sem=recv_sem.at[other],
            device_id=(g, e),
            device_id_type=MESH,
        )

    def reply(e, other):
        return pltpu.make_async_remote_copy(
            src_ref=out_ret.at[e],
            dst_ref=in_ret.at[other],
            send_sem=ret_send_sem.at[e],
            recv_sem=ret_recv_sem.at[other],
            device_id=(g, e),
            device_id_type=MESH,
        )

    cross_message = pltpu.make_async_remote_copy(
        src_ref=out_msg.at[pl.ds(8 * DEVS, 64)],
        dst_ref=in_msg.at[pl.ds(8 * DEVS, 64)],
        send_sem=cross_sem.at[0],
        recv_sem=cross_sem.at[1],
        device_id=(up, d),
        device_id_type=MESH,
    )
    cross_reply = pltpu.make_async_remote_copy(
        src_ref=out_ret.at[pl.ds(DEVS, 8)],
        dst_ref=in_ret.at[pl.ds(DEVS, 8)],
        send_sem=cross_sem.at[2],
        recv_sem=cross_sem.at[3],
        device_id=(down, d),
        device_id_type=MESH,
    )
    own_message = pltpu.make_async_copy(
        out_msg.at[pl.ds(pl.multiple_of(8 * d, 8), ROWS)], in_msg.at[pl.ds(pl.multiple_of(8 * d, 8), ROWS)], recv_sem.at[d]
    )
    own_reply = pltpu.make_async_copy(out_ret.at[d], in_ret.at[d], ret_recv_sem.at[d])

    def octet(t):
        far = (t + 1) // 2
        shift = jnp.where(t % 2 == 1, far, 8 - far)
        return (d // 8 + shift) % 8

    pl.semaphore_wait(barrier, DEVS + 1)
    own_message.start()

    def send_octet(t, _):
        base = 8 * octet(t)

        def send(i, _):
            e = base + (d + i) % 8

            @pl.when(e != d)
            def _():
                message(e, d).start()

            return 0

        lax.fori_loop(0, 8, send, 0)
        return 0

    cross_message.start()
    lax.fori_loop(0, 8, send_octet, 0)

    metas[...] = jnp.zeros_like(metas)
    sums[...] = jnp.zeros_like(sums)
    back[...] = jnp.zeros_like(back)
    lane8 = iota((8, 128), 1)
    lane16 = iota((16, 128), 1)
    per_lane = jnp.where(lane8 < 9, 2.0**-30, jnp.where(lane8 < 12, 2.0**-27, 2.0**-28 / LEVELS))

    def work(t, _):
        is_cross = t == 1
        vg = jnp.where(is_cross, 8, octet(jnp.where(t > 1, t - 1, 0)))

        @pl.when(is_cross)
        def _():
            cross_message.wait_recv()

        @pl.when(t != 1)
        def _():
            def await_one(i, _):
                message(8 * vg + i, 8 * vg + i).wait_recv()
                return 0

            lax.fori_loop(0, 8, await_one, 0)

        at = pl.multiple_of(64 * vg, 64)
        meta = []
        node = []
        for c in range(2):
            row = in_msg[pl.ds(at + 3 * c + 2, 8, stride=8), :].astype(f32) * per_lane
            metas[pl.ds(pl.multiple_of(128 * c + 8 * vg, 8), 8), :] = row
            meta.append(row)
            node.append(cols[pl.ds(pl.multiple_of(128 * c + 8 * vg, 8), 8), :][:, 4:5])
        spread = matmul(jnp.concatenate(parts(jnp.concatenate(meta, axis=0)), axis=1), spread_ref[...])
        mine = (lane16 & 3) == jnp.concatenate(node, axis=0).astype(i32) - 1
        mine = jnp.logical_or(mine, (lane16 & 15) == 12)
        left = jnp.concatenate(
            [jnp.where(mine, spread[:, 128 * k : 128 * k + 128], 0.0) for k in range(3)], axis=0
        ).astype(bf16)
        place = matmul(left, points[...])
        result = jnp.zeros((8, 128), f32)
        for c in range(2):
            even = in_msg[pl.ds(at + 3 * c, 8, stride=8), :]
            odd = in_msg[pl.ds(at + 3 * c + 1, 8, stride=8), :]
            scale = jnp.broadcast_to(jnp.where(node[c] > 0.5, meta[c][:, 12:13], 0.0), (8, 128))
            total = None
            for chunk in range(NODES // 128):
                u = tuple(place[16 * k + 8 * c : 16 * k + 8 * c + 8, 128 * chunk : 128 * chunk + 128] for k in range(3))
                term = contact(even, odd, scale, u)
                total = term if total is None else tuple(a + b for a, b in zip(total, term))
            for n in range(6):
                result = jnp.where(lane8 == 8 * c + n, jnp.sum(total[n], axis=1, keepdims=True), result)
        sums[pl.ds(pl.multiple_of(8 * vg, 8), 8), :] = result
        out_ret[pl.ds(8 * vg, 8), 0, :] = result

        @pl.when(is_cross)
        def _():
            cross_reply.start()

        @pl.when(t != 1)
        def _():
            def answer(i, _):
                e = 8 * vg + i

                @pl.when(e != d)
                def _():
                    reply(e, d).start()

                @pl.when(e == d)
                def _():
                    own_reply.start()

                return 0

            lax.fori_loop(0, 8, answer, 0)

        return 0

    lax.fori_loop(0, 9, work, 0)

    sums_t = sums[...].T
    lane_p = iota((8, 128), 1)
    row_p = iota((8, 128), 0)

    def per_grain(tables, masks):
        out = jnp.zeros((8, 128), f32)
        for grain in range(GRAINS):
            kept = sum(jnp.where(masks[c] == grain + 1.0, tables[c], 0.0) for c in range(2))
            out = jnp.where(lane_p == grain, jnp.sum(kept, axis=1, keepdims=True), out)
        return out

    def stack(rows):
        out = jnp.zeros((8, 128), f32)
        for n, row in enumerate(rows):
            out = jnp.where(row_p == n, row, out)
        return out

    node_tables, node_masks = [], []
    for c in range(2):
        meta_t = metas[128 * c : 128 * c + 128, :].T
        r = [[meta_t[3 * m + k : 3 * m + k + 1, :] for k in range(3)] for m in range(3)]
        mask = attr_rows[4:5, 128 * c : 128 * c + 128]
        centre = []
        for m in range(3):
            value = jnp.zeros((1, 128), f32)
            for grain in range(GRAINS):
                value = jnp.where(mask == grain + 1.0, pose[16 + m : 17 + m, grain : grain + 1], value)
            centre.append(value)
        shift = [r[0][k] * centre[0] + r[1][k] * centre[1] + r[2][k] * centre[2] + meta_t[9 + k : 10 + k, :] for k in range(3)]
        push = [sums_t[8 * c + n : 8 * c + n + 1, :] for n in range(3)]
        twist = [sums_t[8 * c + 3 + n : 8 * c + 4 + n, :] for n in range(3)]
        lever = cross(shift, push)
        twist = [twist[n] - lever[n] for n in range(3)]
        rows = [r[m][0] * v[0] + r[m][1] * v[1] + r[m][2] * v[2] for v in (push, twist) for m in range(3)]
        node_tables.append(stack(rows))
        node_masks.append(mask)
    node_load = per_grain(node_tables, node_masks)

    def await_reply(e, _):
        reply(e, e).wait_recv()
        return 0

    lax.fori_loop(0, DEVS, await_reply, 0)
    cross_reply.wait_recv()
    back[0:TILES, :] = in_ret[:, 0, :]
    back_t = back[...].T
    grid_tables, grid_masks = [], []
    for c in range(2):
        corner = [((GRID - 1) / 2.0 - BASE) - attr_rows[1 + k : 2 + k, 128 * c : 128 * c + 128] for k in range(3)]
        push = [back_t[8 * c + n : 8 * c + n + 1, :] for n in range(3)]
        lever = cross(corner, push)
        twist = [back_t[8 * c + 3 + n : 8 * c + 4 + n, :] - lever[n] for n in range(3)]
        grid_tables.append(stack(push + twist))
        grid_masks.append(attr_rows[0:1, 128 * c : 128 * c + 128])
    grid_load = per_grain(grid_tables, grid_masks)

    def turn(first):
        v = [grid_load[first + k : first + k + 1, 0:GRAINS] for k in range(3)]
        return [rot[3 * m] * v[0] + rot[3 * m + 1] * v[1] + rot[3 * m + 2] * v[2] for m in range(3)]

    force, torque = turn(0), turn(3)
    force = [node_load[m : m + 1, 0:GRAINS] - force[m] for m in range(3)]
    torque = [node_load[3 + m : 4 + m, 0:GRAINS] - torque[m] for m in range(3)]
    mass = mass_ref[...]
    gain = time_step / mass
    spin_gain = time_step / (0.4 * mass * (3.0 * GRID / 16.0) ** 2)
    vel = [velocity_ref[m : m + 1, :] + force[m] * gain for m in range(3)]
    spin = [spin_ref[m : m + 1, :] + torque[m] * spin_gain for m in range(3)]
    for m in range(3):
        new_velocity_ref[m : m + 1, :] = vel[m]
        new_spin_ref[m : m + 1, :] = spin[m]
        new_position_ref[m : m + 1, :] = pos[m] + time_step * vel[m]
    vec = (x, y, z)
    turned = cross(spin, vec)
    quarter = 0.5 * time_step
    q = [w - quarter * (spin[0] * x + spin[1] * y + spin[2] * z)]
    q += [vec[m] + quarter * (w * spin[m] + turned[m]) for m in range(3)]
    norm = jnp.sqrt(q[0] * q[0] + q[1] * q[1] + q[2] * q[2] + q[3] * q[3])
    for k in range(4):
        new_quaternion_ref[k : k + 1, :] = q[k] / norm

    def finish(e, _):
        @pl.when(e != d)
        def _():
            message(e, d).wait_send()
            reply(e, d).wait_send()

        return 0

    lax.fori_loop(0, DEVS, finish, 0)
    cross_message.wait_send()
    cross_reply.wait_send()


ROWS = 6


def body(
    level_set, node_coords, position, quaternion, velocity, spin, mass, grid_slot, brick_anchor, node_slot, grid_cross,
    anchor_cross, node_cross,
):
    vmem = pl.BlockSpec(memory_space=pltpu.VMEM)
    dma = pltpu.SemaphoreType.DMA
    row = lambda a: a.reshape(1, -1)
    outs = pl.pallas_call(
        kernel,
        out_shape=[jax.ShapeDtypeStruct((n, GRAINS), f32) for n in (3, 4, 3, 3)],
        in_specs=[pl.BlockSpec(memory_space=pl.ANY)] + [vmem] * 13,
        out_specs=[vmem] * 4,
        scratch_shapes=[
            pltpu.VMEM((GRAINS, SPAN, 32, GRID), bf16),
            pltpu.VMEM((128, 256), f32),
            pltpu.VMEM((256, 128), f32),
            pltpu.VMEM((384, 128), f32),
            pltpu.VMEM((128, 128), f32),
            pltpu.VMEM((128, NODES), bf16),
            pltpu.VMEM((8 * TILES, 128), i32),
            pltpu.VMEM((8 * TILES, 128), i32),
            pltpu.VMEM((256, 128), f32),
            pltpu.VMEM((128, 128), f32),
            pltpu.VMEM((TILES, 1, 128), f32),
            pltpu.VMEM((TILES, 1, 128), f32),
            pltpu.VMEM((128, 128), f32),
            dma,
            dma((DEVS,)),
            dma((DEVS,)),
            dma((DEVS,)),
            dma((DEVS,)),
            dma((4,)),
        ],
        compiler_params=pltpu.CompilerParams(
            collective_id=0, has_side_effects=True, vmem_limit_bytes=32 * 1024 * 1024
        ),
    )(
        level_set, node_coords, position, quaternion, velocity, spin, row(mass), row(grid_slot), brick_anchor, row(node_slot),
        row(grid_cross), anchor_cross, row(node_cross), jnp.asarray(spread_matrix(), bf16),
    )
    return tuple(outs)


def solution(mesh):
    both = ("group", "dev")
    wide, flat = P(None, both), P(both)
    in_specs = (
        P(both, None, None, None), P(None, both, None), wide, wide, wide, wide, flat, flat, wide, flat, flat, wide, flat,
    )
    return jax.shard_map(body, mesh=mesh, in_specs=in_specs, out_specs=(wide,) * 4, check_vma=False)
```

time: 251 us -> 59.2 us (0.24)
  matrix products: 57.9 us -> 0 us
  waiting for transfers between devices: 54.6 us -> 0 us
  starting transfers between devices: 54 us -> 0 us
  Pallas kernels: 0 us -> 44.5 us
  other arithmetic: 36.9 us -> 0 us
  local copies, waits for them, and re-layouts: 42.4 us -> 13.6 us
    dot_general x45 -> x0, matrix products: 56.3 us -> none  [the longest x9 16.1 us: contact(): jnp.einsum('abc,kan->kbcn', brick_vals.astype(jnp.float32), jnp.stack([ha...]
    all_to_all x4 -> x0, waiting for transfers between devices: 54.6 us -> none  [the longest x1 32.1 us: body(): lax.all_to_all(slot_arms.reshape(dev_count, per_peer, 3, -1), 'dev', spli...]
    all_to_all x4 -> x0, starting transfers between devices: 45.5 us -> none  [the longest x1 18.6 us: body(): lax.all_to_all(slot_valid.reshape(dev_count, per_peer), 'dev', split_axis...]
    pallas_call x0 -> x1, Pallas kernels: none -> 44.5 us  [body(): pl.pallas_call(kernel, out_shape=[jax.ShapeDtypeStruct((n, GRAINS), f32)...]
    reduce_sum x49 -> x0, other arithmetic: 20.2 us -> none  [the longest x9 9.01 us: contact(): along_x = jnp.sum(contracted[1] * hat_y[:, None, :], axis=0)]
    unnamed x34 -> x32, local copies, waits for them, and re-layouts: 4.48 us -> 13.6 us
    dynamic_slice x63 -> x0, local copies, waits for them, and re-layouts: 8.95 us -> none  [contacts_blocked(): return lax.map(run_block, grouped).reshape(-1, 9)]
    ppermute x4 -> x0, starting transfers between devices: 8.48 us -> none  [shifted(): return lax.ppermute(block, axis, route)]
  transfers between devices with their start and end apart: 8 -> 0, of which waited for: 3 -> 0; matrix products, arithmetic and copies ran while one was open for 20% -> 0% of each run, Pallas kernels for 0% -> 0%
where the time goes in v1:
time: 59.2 us; the launch traced here: 58.7 us
  Pallas kernels  44.5 us (75%)
  local copies, waits for them, and re-layouts  13.6 us (23%)
  between operations  0.67 us (1%)
    pallas_call x1, Pallas kernels, body(): pl.pallas_call(kernel, out_shape=[jax.ShapeDtypeStruct((n, GRAINS), f32)...  44.5 us
    unnamed x32, local copies, waits for them, and re-layouts  13.6 us

profile of v1, /device:TPU:24, one launch (start us, length us, event | category | flops | bytes accessed | tf_op | source)
XLA Modules:
  0.0 58.7 jit_solution(16902673896810672917)
XLA Ops:
  0.6 0.0 copy-start
  0.6 2.2 %copy-done = bf16[4,64,64,64]{3,2,1,0:T(8,128)(2,1)S(1)} copy-done((bf16[4,64,64,64]{3,2,1,0:T(8,128)(2,1)S(1)}, bf16[4,64,64,64]{3,2,1,0:T(8,128)(2,1)}, u32[]{:S(2)}) %copy-start) | copy-done | bytes 2097176
  2.8 0.0 copy-start.1
  2.8 1.0 %copy-done.1 = bf16[384,384]{1,0:T(8,128)(2,1)S(1)} copy-done((bf16[384,384]{1,0:T(8,128)(2,1)S(1)}, bf16[384,384]{1,0:T(8,128)(2,1)}, u32[]{:S(2)}) %copy-start.1) | copy-done | bytes 294936
  3.8 0.0 copy-start.2
  3.8 0.7 %copy-done.2 = f32[3,4,512]{2,1,0:T(4,128)S(1)} copy-done((f32[3,4,512]{2,1,0:T(4,128)S(1)}, f32[3,4,512]{2,1,0:T(4,128)}, u32[]{:S(2)}) %copy-start.2) | copy-done | bytes 24600
  4.5 0.0 copy-start.3
  4.5 0.7 %copy-done.3 = f32[3,4]{1,0:T(4,128)S(1)} copy-done((f32[3,4]{1,0:T(4,128)S(1)}, f32[3,4]{1,0:T(4,128)}, u32[]{:S(2)}) %copy-start.3) | copy-done | bytes 72
  5.2 0.0 copy-start.4
  5.2 0.7 %copy-done.4 = f32[4,4]{1,0:T(4,128)S(1)} copy-done((f32[4,4]{1,0:T(4,128)S(1)}, f32[4,4]{1,0:T(4,128)}, u32[]{:S(2)}) %copy-start.4) | copy-done | bytes 88
  5.9 0.0 copy-start.5
  5.9 0.7 %copy-done.5 = f32[3,4]{1,0:T(4,128)S(1)} copy-done((f32[3,4]{1,0:T(4,128)S(1)}, f32[3,4]{1,0:T(4,128)}, u32[]{:S(2)}) %copy-start.5) | copy-done | bytes 72
  6.6 0.0 copy-start.6
  6.6 0.7 %copy-done.6 = f32[3,4]{1,0:T(4,128)S(1)} copy-done((f32[3,4]{1,0:T(4,128)S(1)}, f32[3,4]{1,0:T(4,128)}, u32[]{:S(2)}) %copy-start.6) | copy-done | bytes 72
  7.3 0.0 copy-start.7
  7.3 0.7 %copy-done.7 = s32[3,128]{1,0:T(4,128)S(1)} copy-done((s32[3,128]{1,0:T(4,128)S(1)}, s32[3,128]{1,0:T(4,128)}, u32[]{:S(2)}) %copy-start.7) | copy-done | bytes 1560
  7.9 0.0 copy-start.8
  7.9 0.7 %copy-done.8 = s32[3,16]{1,0:T(4,128)S(1)} copy-done((s32[3,16]{1,0:T(4,128)S(1)}, s32[3,16]{1,0:T(4,128)}, u32[]{:S(2)}) %copy-start.8) | copy-done | bytes 216
  8.6 0.0 copy-start.9
  8.6 0.7 %copy-done.9 = f32[4]{0:T(128)S(1)} copy-done((f32[4]{0:T(128)S(1)}, f32[4]{0:T(128)}, u32[]{:S(2)}) %copy-start.9) | copy-done | bytes 40
  9.3 0.0 copy-start.10
  9.3 0.7 %copy-done.10 = s32[128]{0:T(128)S(1)} copy-done((s32[128]{0:T(128)S(1)}, s32[128]{0:T(128)}, u32[]{:S(2)}) %copy-start.10) | copy-done | bytes 536
  9.9 0.0 copy-start.11
  9.9 0.7 %copy-done.11 = s32[128]{0:T(128)S(1)} copy-done((s32[128]{0:T(128)S(1)}, s32[128]{0:T(128)}, u32[]{:S(2)}) %copy-start.11) | copy-done | bytes 536
  10.6 0.0 copy-start.12
  10.6 0.7 %copy-done.12 = s32[16]{0:T(128)S(1)} copy-done((s32[16]{0:T(128)S(1)}, s32[16]{0:T(128)}, u32[]{:S(2)}) %copy-start.12) | copy-done | bytes 88
  11.2 0.7 %copy-done.13 = s32[16]{0:T(128)S(1)} copy-done((s32[16]{0:T(128)S(1)}, s32[16]{0:T(128)}, u32[]{:S(2)}) %copy-start.13) | copy-done | bytes 88
  11.9 44.5 %shard_map.165 = (f32[3,4]{1,0:T(4,128)S(1)}, f32[4,4]{1,0:T(4,128)S(1)}, f32[3,4]{1,0:T(4,128)S(1)}, f32[3,4]{1,0:T(4,128)S(1)}) custom-call(bf16[4,64,64,64]{3,2,1,0:T(8,128)(2,1)S(1)} %copy-done, f32[3,4,512]{2,1,0:T(4,128)S(1)} %copy-done.2, f32[3,4]{1,0:T(4,128)S(1)} %copy-done.3, f32[4,4]{1,0:T(4,128)S(1)} %copy-done.4, f32[3,4]{1,0:T(4,128)S(1)} %copy-done.5, ...), custom_call_target="tpu_custom_call" | custom-call | tf_op jit(solution)/shard_map/pallas_call | solution.py:502
  56.4 0.6 copy.22
  57.0 0.6 copy.23
  57.6 0.6 copy.24
  58.2 0.6 copy.25
  (1 shorter events, 0.0 us)
Async XLA Ops:
  0.6 2.2 %copy-start = (bf16[4,64,64,64]{3,2,1,0:T(8,128)(2,1)S(1)}, bf16[4,64,64,64]{3,2,1,0:T(8,128)(2,1)}, u32[]{:S(2)}) copy-start(bf16[4,64,64,64]{3,2,1,0:T(8,128)(2,1)} %level_ref.1) | copy-start | bytes 6291460
  2.8 1.0 %copy-start.1 = (bf16[384,384]{1,0:T(8,128)(2,1)S(1)}, bf16[384,384]{1,0:T(8,128)(2,1)}, u32[]{:S(2)}) copy-start(bf16[384,384]{1,0:T(8,128)(2,1)} %constant.2.clone.spread_ref) | copy-start | bytes 884740
  3.8 0.7 %copy-start.2 = (f32[3,4,512]{2,1,0:T(4,128)S(1)}, f32[3,4,512]{2,1,0:T(4,128)}, u32[]{:S(2)}) copy-start(f32[3,4,512]{2,1,0:T(4,128)} %coords_ref.1) | copy-start | bytes 73732
  4.5 0.7 %copy-start.3 = (f32[3,4]{1,0:T(4,128)S(1)}, f32[3,4]{1,0:T(4,128)}, u32[]{:S(2)}) copy-start(f32[3,4]{1,0:T(4,128)} %position_ref.1) | copy-start | bytes 148
  5.2 0.7 %copy-start.4 = (f32[4,4]{1,0:T(4,128)S(1)}, f32[4,4]{1,0:T(4,128)}, u32[]{:S(2)}) copy-start(f32[4,4]{1,0:T(4,128)} %quaternion_ref.1) | copy-start | bytes 196
  5.9 0.7 %copy-start.5 = (f32[3,4]{1,0:T(4,128)S(1)}, f32[3,4]{1,0:T(4,128)}, u32[]{:S(2)}) copy-start(f32[3,4]{1,0:T(4,128)} %velocity_ref.1) | copy-start | bytes 148
  6.6 0.7 %copy-start.6 = (f32[3,4]{1,0:T(4,128)S(1)}, f32[3,4]{1,0:T(4,128)}, u32[]{:S(2)}) copy-start(f32[3,4]{1,0:T(4,128)} %spin_ref.1) | copy-start | bytes 148
  7.3 0.7 %copy-start.7 = (s32[3,128]{1,0:T(4,128)S(1)}, s32[3,128]{1,0:T(4,128)}, u32[]{:S(2)}) copy-start(s32[3,128]{1,0:T(4,128)} %anchor_ref.1) | copy-start | bytes 4612
  7.9 0.7 %copy-start.8 = (s32[3,16]{1,0:T(4,128)S(1)}, s32[3,16]{1,0:T(4,128)}, u32[]{:S(2)}) copy-start(s32[3,16]{1,0:T(4,128)} %anchor_cross_ref.1) | copy-start | bytes 580
  8.6 0.7 %copy-start.9 = (f32[4]{0:T(128)S(1)}, f32[4]{0:T(128)}, u32[]{:S(2)}) copy-start(f32[4]{0:T(128)} %param.20) | copy-start | bytes 52
  9.3 0.7 %copy-start.10 = (s32[128]{0:T(128)S(1)}, s32[128]{0:T(128)}, u32[]{:S(2)}) copy-start(s32[128]{0:T(128)} %param.21) | copy-start | bytes 1540
  9.9 0.7 %copy-start.11 = (s32[128]{0:T(128)S(1)}, s32[128]{0:T(128)}, u32[]{:S(2)}) copy-start(s32[128]{0:T(128)} %param.23) | copy-start | bytes 1540
  10.6 0.7 %copy-start.12 = (s32[16]{0:T(128)S(1)}, s32[16]{0:T(128)}, u32[]{:S(2)}) copy-start(s32[16]{0:T(128)} %param.24) | copy-start | bytes 196
  11.2 0.7 %copy-start.13 = (s32[16]{0:T(128)S(1)}, s32[16]{0:T(128)}, u32[]{:S(2)}) copy-start(s32[16]{0:T(128)} %param.26) | copy-start | bytes 196

commit v2 on v1

--- a/solution.py
+++ b/solution.py
@@ -140,12 +140,19 @@
 
 
 def kernel(
-    level_ref, coords_ref, position_ref, quaternion_ref, velocity_ref, spin_ref, mass_ref, grid_ref, anchor_ref, node_ref,
-    grid_cross_ref, anchor_cross_ref, node_cross_ref, spread_ref,
-    new_position_ref, new_quaternion_ref, new_velocity_ref, new_spin_ref,
-    window, attr, cols, slab, pose, points, out_msg, in_msg, metas, sums, out_ret, in_ret, back,
-    window_sem, send_sem, recv_sem, ret_send_sem, ret_recv_sem, cross_sem,
+    level_ref, *refs
 ):
+    sources, refs = refs[:SMALL], refs[SMALL:]
+    (
+        new_position_ref, new_quaternion_ref, new_velocity_ref, new_spin_ref,
+        window, attr, cols, slab, pose, points, out_msg, in_msg, metas, sums, out_ret, in_ret, back,
+        window_sem, send_sem, recv_sem, ret_send_sem, ret_recv_sem, cross_sem, input_sem,
+    ) = refs[:SCRATCH]
+    inputs = refs[SCRATCH:]
+    (
+        coords_ref, position_ref, quaternion_ref, velocity_ref, spin_ref, mass_ref, grid_ref, anchor_ref, node_ref,
+        grid_cross_ref, anchor_cross_ref, node_cross_ref, spread_ref,
+    ) = inputs
     g = lax.axis_index("group")
     d = lax.axis_index("dev")
     up, down = lax.rem(g + 1, GROUPS), lax.rem(g + GROUPS - 1, GROUPS)
@@ -160,9 +167,18 @@
         level_ref.at[:, BASE : BASE + SPAN, 16:48, :], window, window_sem
     )
     load.start()
+    fetches = [
+        pltpu.make_async_copy(source, target, input_sem.at[n])
+        for n, (source, target) in enumerate(zip(sources, inputs))
+    ]
+    for fetch in fetches:
+        fetch.start()
     lax.fori_loop(1, DEVS, greet, 0)
     for other in (up, down):
         pl.semaphore_signal(barrier, inc=1, device_id=(other, d), device_id_type=MESH)
+
+    for fetch in fetches:
+        fetch.wait()
 
     attr[...] = jnp.zeros_like(attr)
     attr[0:1, 0:128] = (grid_ref[...] + 1).astype(f32)
@@ -490,6 +506,8 @@
 
 
 ROWS = 6
+SMALL = 13
+SCRATCH = 24
 
 
 def body(
@@ -499,10 +517,14 @@
     vmem = pl.BlockSpec(memory_space=pltpu.VMEM)
     dma = pltpu.SemaphoreType.DMA
     row = lambda a: a.reshape(1, -1)
+    small = (
+        node_coords, position, quaternion, velocity, spin, row(mass), row(grid_slot), brick_anchor, row(node_slot),
+        row(grid_cross), anchor_cross, row(node_cross), jnp.asarray(spread_matrix(), bf16),
+    )
     outs = pl.pallas_call(
         kernel,
         out_shape=[jax.ShapeDtypeStruct((n, GRAINS), f32) for n in (3, 4, 3, 3)],
-        in_specs=[pl.BlockSpec(memory_space=pl.ANY)] + [vmem] * 13,
+        in_specs=[pl.BlockSpec(memory_space=pl.ANY)] * (1 + SMALL),
         out_specs=[vmem] * 4,
         scratch_shapes=[
             pltpu.VMEM((GRAINS, SPAN, 32, GRID), bf16),
@@ -524,14 +546,13 @@
             dma((DEVS,)),
             dma((DEVS,)),
             dma((4,)),
-        ],
+            dma((SMALL,)),
+        ]
+        + [pltpu.VMEM(a.shape, a.dtype) for a in small],
         compiler_params=pltpu.CompilerParams(
-            collective_id=0, has_side_effects=True, vmem_limit_bytes=32 * 1024 * 1024
+            collective_id=0, has_side_effects=True, vmem_limit_bytes=60 * 1024 * 1024
         ),
-    )(
-        level_set, node_coords, position, quaternion, velocity, spin, row(mass), row(grid_slot), brick_anchor, row(node_slot),
-        row(grid_cross), anchor_cross, row(node_cross), jnp.asarray(spread_matrix(), bf16),
-    )
+    )(level_set, *small)
     return tuple(outs)
 
 

time: 59.2 us -> 51.4 us (0.87)
  local copies, waits for them, and re-layouts: 13.6 us -> 4.96 us
  Pallas kernels: 44.5 us -> 45.6 us
    unnamed x32 -> x4, local copies, waits for them, and re-layouts: 13.6 us -> 4.96 us
    pallas_call x1, Pallas kernels: 44.5 us -> 45.6 us  [body(): pl.pallas_call(kernel, out_shape=[jax.ShapeDtypeStruct((n, GRAINS), f32)...]
where the time goes in v2:
time: 51.4 us; the launch traced here: 51.2 us
  Pallas kernels  45.6 us (89%)
  local copies, waits for them, and re-layouts  4.96 us (10%)
  between operations  0.65 us (1%)
    pallas_call x1, Pallas kernels, body(): pl.pallas_call(kernel, out_shape=[jax.ShapeDtypeStruct((n, GRAINS), f32)...  45.6 us
    unnamed x4, local copies, waits for them, and re-layouts  4.96 us

profile of v2, /device:TPU:24, one launch (start us, length us, event | category | flops | bytes accessed | tf_op | source)
XLA Modules:
  0.0 51.2 jit_solution(7865409332368681827)
XLA Ops:
  0.6 45.6 %shard_map.165 = (f32[3,4]{1,0:T(4,128)}, f32[4,4]{1,0:T(4,128)}, f32[3,4]{1,0:T(4,128)}, f32[3,4]{1,0:T(4,128)}) custom-call(bf16[4,64,64,64]{3,2,1,0:T(8,128)(2,1)} %level_ref.1, f32[3,4,512]{2,1,0:T(4,128)} %refs_0_.1, f32[3,4]{1,0:T(4,128)} %refs_1_.1, f32[4,4]{1,0:T(4,128)} %refs_2_.1, f32[3,4]{1,0:T(4,128)} %refs_3_.1, f32[3,4]{1,0:T(4,128)} %refs_4_.1, ...), custom_call_target="tpu_custom_call" | custom-call | tf_op jit(solution)/shard_map/pallas_call | solution.py:524
  46.2 1.2 %copy.22 = f32[3,4]{1,0:T(4,128)} copy(f32[3,4]{1,0:T(4,128)} %get-tuple-element.8) | data formatting | bytes 96
  47.4 1.2 %copy.23 = f32[4,4]{1,0:T(4,128)} copy(f32[4,4]{1,0:T(4,128)} %get-tuple-element.9) | data formatting | bytes 128
  48.7 1.2 %copy.24 = f32[3,4]{1,0:T(4,128)} copy(f32[3,4]{1,0:T(4,128)} %get-tuple-element.10) | data formatting | bytes 96
  49.9 1.2 %copy.25 = f32[3,4]{1,0:T(4,128)} copy(f32[3,4]{1,0:T(4,128)} %get-tuple-element.11) | data formatting | bytes 96

commit v3 on v2

--- a/solution.py
+++ b/solution.py
@@ -1,6 +1,5 @@
 import jax
 import jax.numpy as jnp
-import numpy as np
 from jax import lax
 from jax.experimental import pallas as pl
 from jax.experimental.pallas import tpu as pltpu
@@ -21,19 +20,8 @@
 LEVELS = 32766.0
 stiffness = 0.1
 time_step = 0.5
-R_PART = (0, 0, 1, 1, 0, 2)
-P_PART = (0, 1, 0, 1, 2, 0)
-
-
-def spread_matrix():
-    spread = np.zeros((3 * 128, 3 * 128), np.float32)
-    for k in range(3):
-        for combo, part in enumerate(R_PART):
-            for m in range(3):
-                for grain in range(GRAINS):
-                    spread[128 * part + 3 * m + k, 128 * k + 16 * combo + 4 * m + grain] = 1.0
-            spread[128 * part + 9 + k, 128 * k + 16 * combo + 12] = 1.0
-    return spread
+R_PART = (0, 0, 1, 1)
+P_PART = (0, 1, 0, 1)
 
 
 def iota(shape, dim):
@@ -145,13 +133,13 @@
     sources, refs = refs[:SMALL], refs[SMALL:]
     (
         new_position_ref, new_quaternion_ref, new_velocity_ref, new_spin_ref,
-        window, attr, cols, slab, pose, points, out_msg, in_msg, metas, sums, out_ret, in_ret, back,
+        window, attr, cols, slab, pose, points, out_msg, in_msg, metas, sums, back,
         window_sem, send_sem, recv_sem, ret_send_sem, ret_recv_sem, cross_sem, input_sem,
     ) = refs[:SCRATCH]
     inputs = refs[SCRATCH:]
     (
         coords_ref, position_ref, quaternion_ref, velocity_ref, spin_ref, mass_ref, grid_ref, anchor_ref, node_ref,
-        grid_cross_ref, anchor_cross_ref, node_cross_ref, spread_ref,
+        grid_cross_ref, anchor_cross_ref, node_cross_ref,
     ) = inputs
     g = lax.axis_index("group")
     d = lax.axis_index("dev")
@@ -173,7 +161,7 @@
     ]
     for fetch in fetches:
         fetch.start()
-    lax.fori_loop(1, DEVS, greet, 0)
+    lax.fori_loop(1, DEVS, greet, 0, unroll=7)
     for other in (up, down):
         pl.semaphore_signal(barrier, inc=1, device_id=(other, d), device_id_type=MESH)
 
@@ -190,7 +178,6 @@
     slot_to = iota((256, 256), 0)
     order = (iota((256, 256), 1) == ((slot_to & 127) << 1) + (slot_to >> 7)).astype(f32).astype(bf16)
     attr_b = attr[...].astype(bf16)
-    attr_rows = matmul_nt(attr_b, order)
     cols[...] = matmul_nt(order, attr_b)
 
     w, x, y, z = (quaternion_ref[k : k + 1, :] for k in range(4))
@@ -201,25 +188,15 @@
     )
     pos = [position_ref[m : m + 1, :] for m in range(3)]
     pose[...] = jnp.zeros_like(pose)
-    for n in range(9):
-        pose[n : n + 1, 0:GRAINS] = rot[n]
     for k in range(3):
         turned = rot[k] * pos[0] + rot[3 + k] * pos[1] + rot[6 + k] * pos[2]
-        pose[9 + k : 10 + k, 0:GRAINS] = ((GRID - 1) / 2.0 - BASE) - turned
-        pose[16 + k : 17 + k, 0:GRAINS] = pos[k]
+        for half in (0, 64):
+            at = half + 16 * k
+            for m in range(3):
+                pose[at + 4 * m : at + 4 * m + 4, 0:GRAINS] = jnp.broadcast_to(rot[3 * m + k], (4, GRAINS))
+            pose[at + 12 : at + 13, 0:GRAINS] = ((GRID - 1) / 2.0 - BASE) - turned
+            pose[at + 14 : at + 15, 0:GRAINS] = pos[k]
     pose_cols = pose[...].T
-
-    points[...] = jnp.zeros_like(points)
-    world = []
-    for m in range(3):
-        p = pose_cols[0:GRAINS, 16 + m : 17 + m]
-        for n in range(3):
-            p = p + pose_cols[0:GRAINS, 3 * m + n : 3 * m + n + 1] * coords_ref[n]
-        world.append(p)
-    ones = jnp.where(iota((GRAINS, NODES), 0) == 0, 1.0, 0.0)
-    world = parts(jnp.concatenate(world + [ones], axis=0))
-    for combo, part in enumerate(P_PART):
-        points[16 * combo : 16 * combo + 16, :] = world[part]
 
     lane64 = iota((64, 384), 1)
     select_z = (iota((64, 384), 0) == BASE + (lane64 >> 7) + (lane64 & 7)).astype(f32).astype(bf16)
@@ -247,7 +224,11 @@
     bricks = matmul(pick, slab[...].astype(bf16))
     lane = iota((TILES, 128), 1)
     pose_parts = parts(pose_cols)
-    unit = jnp.where(lane < 9, 2.0**30, jnp.where(lane < 12, 2.0**27, 2.0**28))
+    lane_f = lane & 15
+    unit = jnp.where(
+        lane_f < 12, 2.0**30, jnp.where(lane_f == 12, 2.0**27, jnp.where(lane_f == 13, 2.0**28, 0.0))
+    )
+    halves = []
     for c in range(2):
         rows = [bricks[TILES * (4 * c + j) : TILES * (4 * c + j + 1), :] for j in range(4)]
         most = jnp.maximum(
@@ -256,33 +237,53 @@
         most = jnp.maximum(jnp.max(most, axis=1, keepdims=True), 1e-6)
         inverse = LEVELS / most
         level = [jnp.floor(row * inverse + 0.5).astype(i32) for row in rows]
-        out_msg[pl.ds(3 * c, TILES, stride=8), :] = (level[1] << 16) + level[0]
-        out_msg[pl.ds(3 * c + 1, TILES, stride=8), :] = (level[3] << 16) + level[2]
+        out_msg[pl.ds(2 * c, TILES, stride=8), :] = (level[1] << 16) + level[0]
+        out_msg[pl.ds(2 * c + 1, TILES, stride=8), :] = (level[3] << 16) + level[2]
         own = cols[128 * c : 128 * c + TILES, :]
         grain = (own[:, 0:1].astype(i32) - 1 == lane).astype(f32).astype(bf16)
         meta = matmul(grain, pose_parts[0]) + matmul(grain, pose_parts[1]) + matmul(grain, pose_parts[2])
         for k in range(3):
-            meta = meta - jnp.where(lane == 9 + k, own[:, 1 + k : 2 + k], 0.0)
-        meta = jnp.where(lane == 12, most, jnp.where(lane < 12, meta, 0.0))
-        out_msg[pl.ds(3 * c + 2, TILES, stride=8), :] = (meta * unit).astype(i32)
+            meta = meta - jnp.where(lane == 64 * c + 16 * k + 12, own[:, 1 + k : 2 + k], 0.0)
+        halves.append(jnp.where(lane_f == 13, most, meta))
+    out_msg[pl.ds(4, TILES, stride=8), :] = (jnp.where(lane < 64, halves[0], halves[1]) * unit).astype(i32)
 
     def message(e, other):
         return pltpu.make_async_remote_copy(
             src_ref=out_msg.at[pl.ds(pl.multiple_of(8 * e, 8), ROWS)],
             dst_ref=in_msg.at[pl.ds(pl.multiple_of(8 * other, 8), ROWS)],
-            send_sem=send_sem.at[e],
-            recv_sem=recv_sem.at[other],
+            send_sem=send_sem,
+            recv_sem=recv_sem.at[other // 8],
             device_id=(g, e),
             device_id_type=MESH,
         )
 
+    def messages(count, octet):
+        return pltpu.make_async_remote_copy(
+            src_ref=out_msg.at[pl.ds(0, ROWS * count)],
+            dst_ref=in_msg.at[pl.ds(0, ROWS * count)],
+            send_sem=send_sem,
+            recv_sem=recv_sem.at[octet],
+            device_id=(up, d),
+            device_id_type=MESH,
+        )
+
     def reply(e, other):
         return pltpu.make_async_remote_copy(
-            src_ref=out_ret.at[e],
-            dst_ref=in_ret.at[other],
-            send_sem=ret_send_sem.at[e],
-            recv_sem=ret_recv_sem.at[other],
+            src_ref=sums.at[pl.ds(e, 1)],
+            dst_ref=back.at[pl.ds(other, 1)],
+            send_sem=ret_send_sem,
+            recv_sem=ret_recv_sem,
             device_id=(g, e),
+            device_id_type=MESH,
+        )
+
+    def replies(count):
+        return pltpu.make_async_remote_copy(
+            src_ref=sums.at[pl.ds(0, count)],
+            dst_ref=back.at[pl.ds(0, count)],
+            send_sem=ret_send_sem,
+            recv_sem=ret_recv_sem,
+            device_id=(up, d),
             device_id_type=MESH,
         )
 
@@ -295,50 +296,58 @@
         device_id_type=MESH,
     )
     cross_reply = pltpu.make_async_remote_copy(
-        src_ref=out_ret.at[pl.ds(DEVS, 8)],
-        dst_ref=in_ret.at[pl.ds(DEVS, 8)],
+        src_ref=sums.at[pl.ds(DEVS, 8)],
+        dst_ref=back.at[pl.ds(DEVS, 8)],
         send_sem=cross_sem.at[2],
         recv_sem=cross_sem.at[3],
         device_id=(down, d),
         device_id_type=MESH,
     )
-    own_message = pltpu.make_async_copy(
-        out_msg.at[pl.ds(pl.multiple_of(8 * d, 8), ROWS)], in_msg.at[pl.ds(pl.multiple_of(8 * d, 8), ROWS)], recv_sem.at[d]
-    )
-    own_reply = pltpu.make_async_copy(out_ret.at[d], in_ret.at[d], ret_recv_sem.at[d])
+    own = d // 8
+    own_rows = pl.ds(pl.multiple_of(8 * d, 8), ROWS)
+    own_message = pltpu.make_async_copy(out_msg.at[own_rows], in_msg.at[own_rows], recv_sem.at[own])
+    own_reply = pltpu.make_async_copy(sums.at[pl.ds(d, 1)], back.at[pl.ds(d, 1)], ret_recv_sem)
 
     def octet(t):
         far = (t + 1) // 2
         shift = jnp.where(t % 2 == 1, far, 8 - far)
-        return (d // 8 + shift) % 8
-
+        return (own + shift) % 8
+
+    metas[...] = jnp.zeros_like(metas)
+    sums[...] = jnp.zeros_like(sums)
+    back[TILES:128, :] = jnp.zeros((128 - TILES, 128), f32)
     pl.semaphore_wait(barrier, DEVS + 1)
     own_message.start()
+    for i in range(1, 8):
+        message(8 * own + (d + i) % 8, d).start()
+    cross_message.start()
 
     def send_octet(t, _):
         base = 8 * octet(t)
-
-        def send(i, _):
-            e = base + (d + i) % 8
-
-            @pl.when(e != d)
-            def _():
-                message(e, d).start()
-
-            return 0
-
-        lax.fori_loop(0, 8, send, 0)
+        for i in range(8):
+            message(base + (d + i) % 8, d).start()
         return 0
 
-    cross_message.start()
-    lax.fori_loop(0, 8, send_octet, 0)
-
-    metas[...] = jnp.zeros_like(metas)
-    sums[...] = jnp.zeros_like(sums)
-    back[...] = jnp.zeros_like(back)
+    lax.fori_loop(1, 8, send_octet, 0)
+
+    world = []
+    for m in range(3):
+        p = pose_cols[0:GRAINS, 16 * m + 14 : 16 * m + 15]
+        for n in range(3):
+            lane_r = 16 * n + 4 * m
+            p = p + pose_cols[0:GRAINS, lane_r : lane_r + 1] * coords_ref[n]
+        world.append(p)
+    ones = jnp.where(iota((GRAINS, NODES), 0) == 0, 1.0, 0.0)
+    world = parts(jnp.concatenate(world + [ones], axis=0))
+    for combo, part in enumerate(P_PART):
+        for block in range(8):
+            points[128 * combo + 16 * block : 128 * combo + 16 * block + 16, :] = world[part]
+    attr_rows = matmul_nt(attr_b, order)
     lane8 = iota((8, 128), 1)
-    lane16 = iota((16, 128), 1)
-    per_lane = jnp.where(lane8 < 9, 2.0**-30, jnp.where(lane8 < 12, 2.0**-27, 2.0**-28 / LEVELS))
+    lane8_f = lane8 & 15
+    per_lane = jnp.where(
+        lane8_f < 12, 2.0**-30, jnp.where(lane8_f == 12, 2.0**-27, jnp.where(lane8_f == 13, 2.0**-28 / LEVELS, 0.0))
+    )
 
     def work(t, _):
         is_cross = t == 1
@@ -350,32 +359,23 @@
 
         @pl.when(t != 1)
         def _():
-            def await_one(i, _):
-                message(8 * vg + i, 8 * vg + i).wait_recv()
-                return 0
-
-            lax.fori_loop(0, 8, await_one, 0)
+            messages(8, vg).wait_recv()
 
         at = pl.multiple_of(64 * vg, 64)
-        meta = []
-        node = []
-        for c in range(2):
-            row = in_msg[pl.ds(at + 3 * c + 2, 8, stride=8), :].astype(f32) * per_lane
-            metas[pl.ds(pl.multiple_of(128 * c + 8 * vg, 8), 8), :] = row
-            meta.append(row)
-            node.append(cols[pl.ds(pl.multiple_of(128 * c + 8 * vg, 8), 8), :][:, 4:5])
-        spread = matmul(jnp.concatenate(parts(jnp.concatenate(meta, axis=0)), axis=1), spread_ref[...])
-        mine = (lane16 & 3) == jnp.concatenate(node, axis=0).astype(i32) - 1
-        mine = jnp.logical_or(mine, (lane16 & 15) == 12)
-        left = jnp.concatenate(
-            [jnp.where(mine, spread[:, 128 * k : 128 * k + 128], 0.0) for k in range(3)], axis=0
-        ).astype(bf16)
-        place = matmul(left, points[...])
+        meta = in_msg[pl.ds(at + 4, 8, stride=8), :].astype(f32) * per_lane
+        metas[pl.ds(pl.multiple_of(8 * vg, 8), 8), :] = meta
+        node = [cols[pl.ds(pl.multiple_of(128 * c + 8 * vg, 8), 8), :][:, 4:5] for c in range(2)]
+        mine = [jnp.logical_or((lane8 & 3) == node[c].astype(i32) - 1, lane8_f == 12) for c in range(2)]
+        left = [
+            jnp.where(jnp.logical_and(mine[c], (lane8 >> 4) == 4 * c + k), meta, 0.0) for k in range(3) for c in range(2)
+        ]
+        left = parts(jnp.concatenate(left, axis=0))
+        place = matmul(jnp.concatenate([left[part] for part in R_PART], axis=1), points[...])
         result = jnp.zeros((8, 128), f32)
         for c in range(2):
-            even = in_msg[pl.ds(at + 3 * c, 8, stride=8), :]
-            odd = in_msg[pl.ds(at + 3 * c + 1, 8, stride=8), :]
-            scale = jnp.broadcast_to(jnp.where(node[c] > 0.5, meta[c][:, 12:13], 0.0), (8, 128))
+            even = in_msg[pl.ds(at + 2 * c, 8, stride=8), :]
+            odd = in_msg[pl.ds(at + 2 * c + 1, 8, stride=8), :]
+            scale = jnp.broadcast_to(jnp.where(node[c] > 0.5, meta[:, 64 * c + 13 : 64 * c + 14], 0.0), (8, 128))
             total = None
             for chunk in range(NODES // 128):
                 u = tuple(place[16 * k + 8 * c : 16 * k + 8 * c + 8, 128 * chunk : 128 * chunk + 128] for k in range(3))
@@ -384,28 +384,21 @@
             for n in range(6):
                 result = jnp.where(lane8 == 8 * c + n, jnp.sum(total[n], axis=1, keepdims=True), result)
         sums[pl.ds(pl.multiple_of(8 * vg, 8), 8), :] = result
-        out_ret[pl.ds(8 * vg, 8), 0, :] = result
 
         @pl.when(is_cross)
         def _():
             cross_reply.start()
 
-        @pl.when(t != 1)
+        @pl.when(t == 0)
         def _():
-            def answer(i, _):
-                e = 8 * vg + i
-
-                @pl.when(e != d)
-                def _():
-                    reply(e, d).start()
-
-                @pl.when(e == d)
-                def _():
-                    own_reply.start()
-
-                return 0
-
-            lax.fori_loop(0, 8, answer, 0)
+            own_reply.start()
+            for i in range(1, 8):
+                reply(8 * vg + (d + i) % 8, d).start()
+
+        @pl.when(t > 1)
+        def _():
+            for i in range(8):
+                reply(8 * vg + (d + i) % 8, d).start()
 
         return 0
 
@@ -428,18 +421,22 @@
             out = jnp.where(row_p == n, row, out)
         return out
 
+    meta_t = metas[...].T
     node_tables, node_masks = [], []
     for c in range(2):
-        meta_t = metas[128 * c : 128 * c + 128, :].T
-        r = [[meta_t[3 * m + k : 3 * m + k + 1, :] for k in range(3)] for m in range(3)]
+        at = 64 * c
+        r = [[meta_t[at + 16 * k + 4 * m : at + 16 * k + 4 * m + 1, :] for k in range(3)] for m in range(3)]
         mask = attr_rows[4:5, 128 * c : 128 * c + 128]
         centre = []
         for m in range(3):
             value = jnp.zeros((1, 128), f32)
             for grain in range(GRAINS):
-                value = jnp.where(mask == grain + 1.0, pose[16 + m : 17 + m, grain : grain + 1], value)
+                value = jnp.where(mask == grain + 1.0, pose[16 * m + 14 : 16 * m + 15, grain : grain + 1], value)
             centre.append(value)
-        shift = [r[0][k] * centre[0] + r[1][k] * centre[1] + r[2][k] * centre[2] + meta_t[9 + k : 10 + k, :] for k in range(3)]
+        shift = [
+            r[0][k] * centre[0] + r[1][k] * centre[1] + r[2][k] * centre[2] + meta_t[at + 16 * k + 12 : at + 16 * k + 13, :]
+            for k in range(3)
+        ]
         push = [sums_t[8 * c + n : 8 * c + n + 1, :] for n in range(3)]
         twist = [sums_t[8 * c + 3 + n : 8 * c + 4 + n, :] for n in range(3)]
         lever = cross(shift, push)
@@ -449,13 +446,8 @@
         node_masks.append(mask)
     node_load = per_grain(node_tables, node_masks)
 
-    def await_reply(e, _):
-        reply(e, e).wait_recv()
-        return 0
-
-    lax.fori_loop(0, DEVS, await_reply, 0)
+    replies(DEVS).wait_recv()
     cross_reply.wait_recv()
-    back[0:TILES, :] = in_ret[:, 0, :]
     back_t = back[...].T
     grid_tables, grid_masks = [], []
     for c in range(2):
@@ -492,22 +484,35 @@
     for k in range(4):
         new_quaternion_ref[k : k + 1, :] = q[k] / norm
 
-    def finish(e, _):
-        @pl.when(e != d)
-        def _():
-            message(e, d).wait_send()
-            reply(e, d).wait_send()
-
-        return 0
-
-    lax.fori_loop(0, DEVS, finish, 0)
+    messages(DEVS - 1, 0).wait_send()
+    replies(DEVS - 1).wait_send()
     cross_message.wait_send()
     cross_reply.wait_send()
 
 
-ROWS = 6
-SMALL = 13
-SCRATCH = 24
+ROWS = 5
+SMALL = 12
+SCRATCH = 22
+
+
+def settle_kernel(*refs):
+    sem = refs[8]
+    copies = [pltpu.make_async_copy(refs[n], refs[4 + n], sem.at[n]) for n in range(4)]
+    for copy in copies:
+        copy.start()
+    for copy in copies:
+        copy.wait()
+
+
+def settle(outs):
+    anywhere = pl.BlockSpec(memory_space=pl.ANY)
+    return pl.pallas_call(
+        settle_kernel,
+        out_shape=[jax.ShapeDtypeStruct(a.shape, a.dtype) for a in outs],
+        in_specs=[anywhere] * 4,
+        out_specs=[anywhere] * 4,
+        scratch_shapes=[pltpu.SemaphoreType.DMA((4,))],
+    )(*outs)
 
 
 def body(
@@ -519,7 +524,7 @@
     row = lambda a: a.reshape(1, -1)
     small = (
         node_coords, position, quaternion, velocity, spin, row(mass), row(grid_slot), brick_anchor, row(node_slot),
-        row(grid_cross), anchor_cross, row(node_cross), jnp.asarray(spread_matrix(), bf16),
+        row(grid_cross), anchor_cross, row(node_cross),
     )
     outs = pl.pallas_call(
         kernel,
@@ -532,19 +537,17 @@
             pltpu.VMEM((256, 128), f32),
             pltpu.VMEM((384, 128), f32),
             pltpu.VMEM((128, 128), f32),
-            pltpu.VMEM((128, NODES), bf16),
+            pltpu.VMEM((128 * len(P_PART), NODES), bf16),
             pltpu.VMEM((8 * TILES, 128), i32),
             pltpu.VMEM((8 * TILES, 128), i32),
-            pltpu.VMEM((256, 128), f32),
             pltpu.VMEM((128, 128), f32),
-            pltpu.VMEM((TILES, 1, 128), f32),
-            pltpu.VMEM((TILES, 1, 128), f32),
+            pltpu.VMEM((128, 128), f32),
             pltpu.VMEM((128, 128), f32),
             dma,
-            dma((DEVS,)),
-            dma((DEVS,)),
-            dma((DEVS,)),
-            dma((DEVS,)),
+            dma,
+            dma((8,)),
+            dma,
+            dma,
             dma((4,)),
             dma((SMALL,)),
         ]
@@ -553,7 +556,7 @@
             collective_id=0, has_side_effects=True, vmem_limit_bytes=60 * 1024 * 1024
         ),
     )(level_set, *small)
-    return tuple(outs)
+    return tuple(settle(outs))
 
 
 def solution(mesh):

time: 51.4 us -> 43.5 us (0.85)
  local copies, waits for them, and re-layouts: 4.96 us -> 0 us
  Pallas kernels: 45.6 us -> 42.7 us
    unnamed x4 -> x0, local copies, waits for them, and re-layouts: 4.96 us -> none
    pallas_call x1, Pallas kernels: 45.6 us -> 41.3 us  [body(): pl.pallas_call(kernel, out_shape=[jax.ShapeDtypeStruct((n, GRAINS), f32)...]
    pallas_call x0 -> x1, Pallas kernels: none -> 1.34 us  [settle(): pl.pallas_call(settle_kernel, out_shape=[jax.ShapeDtypeStruct(a.shape, a....]
where the time goes in v3:
time: 43.5 us; the launch traced here: 43.3 us
  Pallas kernels  42.7 us (98%)
  between operations  0.64 us (1%)
    pallas_call x1, Pallas kernels, body(): pl.pallas_call(kernel, out_shape=[jax.ShapeDtypeStruct((n, GRAINS), f32)...  41.3 us
    pallas_call x1, Pallas kernels, settle(): pl.pallas_call(settle_kernel, out_shape=[jax.ShapeDtypeStruct(a.shape, a....  1.34 us

profile of v3, /device:TPU:24, one launch (start us, length us, event | category | flops | bytes accessed | tf_op | source)
XLA Modules:
  0.0 43.3 jit_solution(16919822512395266968)
XLA Ops:
  0.6 41.3 %shard_map.156 = (f32[3,4]{1,0:T(4,128)}, f32[4,4]{1,0:T(4,128)}, f32[3,4]{1,0:T(4,128)}, f32[3,4]{1,0:T(4,128)}) custom-call(bf16[4,64,64,64]{3,2,1,0:T(8,128)(2,1)} %level_ref.1, f32[3,4,512]{2,1,0:T(4,128)} %refs_0_.1, f32[3,4]{1,0:T(4,128)} %refs_1_.1, f32[4,4]{1,0:T(4,128)} %refs_2_.1, f32[3,4]{1,0:T(4,128)} %refs_3_.1, f32[3,4]{1,0:T(4,128)} %refs_4_.1, ...), custom_call_target="tpu_custom_call" | custom-call | tf_op jit(solution)/shard_map/pallas_call | solution.py:529
  42.0 1.3 %shard_map.157 = (f32[3,4]{1,0:T(4,128)}, f32[4,4]{1,0:T(4,128)}, f32[3,4]{1,0:T(4,128)}, f32[3,4]{1,0:T(4,128)}) custom-call(f32[3,4]{1,0:T(4,128)} %get-tuple-element.8.refs_0_, f32[4,4]{1,0:T(4,128)} %get-tuple-element.9.refs_1_, f32[3,4]{1,0:T(4,128)} %get-tuple-element.10.refs_2_, f32[3,4]{1,0:T(4,128)} %get-tuple-element.11.refs_3_), custom_call_target="tpu_custom_call" | custom-call | tf_op jit(solution)/shard_map/pallas_call | solution.py:509

commit v4 on v3

--- a/solution.py
+++ b/solution.py
@@ -161,7 +161,13 @@
     ]
     for fetch in fetches:
         fetch.start()
-    lax.fori_loop(1, DEVS, greet, 0, unroll=7)
+    greet(DEVS // 2, 0)
+
+    def greet_two(j, _):
+        greet(DEVS // 2 - j, 0)
+        return greet(DEVS // 2 + j, 0)
+
+    lax.fori_loop(1, DEVS // 2, greet_two, 0, unroll=4)
     for other in (up, down):
         pl.semaphore_signal(barrier, inc=1, device_id=(other, d), device_id_type=MESH)
 
@@ -317,18 +323,18 @@
     sums[...] = jnp.zeros_like(sums)
     back[TILES:128, :] = jnp.zeros((128 - TILES, 128), f32)
     pl.semaphore_wait(barrier, DEVS + 1)
+
+    def send_octet(t, _):
+        base = 8 * octet(8 - t)
+        for i in range(8):
+            message(base + (d + i) % 8, d).start()
+        return 0
+
+    lax.fori_loop(1, 8, send_octet, 0)
     own_message.start()
     for i in range(1, 8):
         message(8 * own + (d + i) % 8, d).start()
     cross_message.start()
-
-    def send_octet(t, _):
-        base = 8 * octet(t)
-        for i in range(8):
-            message(base + (d + i) % 8, d).start()
-        return 0
-
-    lax.fori_loop(1, 8, send_octet, 0)
 
     world = []
     for m in range(3):
@@ -351,7 +357,7 @@
 
     def work(t, _):
         is_cross = t == 1
-        vg = jnp.where(is_cross, 8, octet(jnp.where(t > 1, t - 1, 0)))
+        vg = jnp.where(is_cross, 8, octet(jnp.where(t > 1, 9 - t, 0)))
 
         @pl.when(is_cross)
         def _():

time: 43.5 us -> 40.7 us (0.936)
  Pallas kernels: 42.7 us -> 39.9 us
    pallas_call x1, Pallas kernels: 41.3 us -> 38.6 us  [body(): pl.pallas_call(kernel, out_shape=[jax.ShapeDtypeStruct((n, GRAINS), f32)...]
where the time goes in v4:
time: 40.7 us; the launch traced here: 40.6 us
  Pallas kernels  39.9 us (98%)
  between operations  0.64 us (2%)
    pallas_call x1, Pallas kernels, body(): pl.pallas_call(kernel, out_shape=[jax.ShapeDtypeStruct((n, GRAINS), f32)...  38.6 us
    pallas_call x1, Pallas kernels, settle(): pl.pallas_call(settle_kernel, out_shape=[jax.ShapeDtypeStruct(a.shape, a....  1.34 us

profile of v4, /device:TPU:24, one launch (start us, length us, event | category | flops | bytes accessed | tf_op | source)
XLA Modules:
  0.0 40.6 jit_solution(9631807912727941030)
XLA Ops:
  0.6 38.6 %shard_map.156 = (f32[3,4]{1,0:T(4,128)}, f32[4,4]{1,0:T(4,128)}, f32[3,4]{1,0:T(4,128)}, f32[3,4]{1,0:T(4,128)}) custom-call(bf16[4,64,64,64]{3,2,1,0:T(8,128)(2,1)} %level_ref.1, f32[3,4,512]{2,1,0:T(4,128)} %refs_0_.1, f32[3,4]{1,0:T(4,128)} %refs_1_.1, f32[4,4]{1,0:T(4,128)} %refs_2_.1, f32[3,4]{1,0:T(4,128)} %refs_3_.1, f32[3,4]{1,0:T(4,128)} %refs_4_.1, ...), custom_call_target="tpu_custom_call" | custom-call | tf_op jit(solution)/shard_map/pallas_call | solution.py:535
  39.2 1.3 %shard_map.157 = (f32[3,4]{1,0:T(4,128)}, f32[4,4]{1,0:T(4,128)}, f32[3,4]{1,0:T(4,128)}, f32[3,4]{1,0:T(4,128)}) custom-call(f32[3,4]{1,0:T(4,128)} %get-tuple-element.8.refs_0_, f32[4,4]{1,0:T(4,128)} %get-tuple-element.9.refs_1_, f32[3,4]{1,0:T(4,128)} %get-tuple-element.10.refs_2_, f32[3,4]{1,0:T(4,128)} %get-tuple-element.11.refs_3_), custom_call_target="tpu_custom_call" | custom-call | tf_op jit(solution)/shard_map/pallas_call | solution.py:515

commit v5 on v4

--- a/solution.py
+++ b/solution.py
@@ -132,7 +132,7 @@
 ):
     sources, refs = refs[:SMALL], refs[SMALL:]
     (
-        new_position_ref, new_quaternion_ref, new_velocity_ref, new_spin_ref,
+        out_ref,
         window, attr, cols, slab, pose, points, out_msg, in_msg, metas, sums, back,
         window_sem, send_sem, recv_sem, ret_send_sem, ret_recv_sem, cross_sem, input_sem,
     ) = refs[:SCRATCH]
@@ -356,14 +356,14 @@
     )
 
     def work(t, _):
-        is_cross = t == 1
-        vg = jnp.where(is_cross, 8, octet(jnp.where(t > 1, 9 - t, 0)))
+        is_cross = t == 8
+        vg = jnp.where(is_cross, 8, octet(jnp.where(t > 0, 8 - t, 0)))
 
         @pl.when(is_cross)
         def _():
             cross_message.wait_recv()
 
-        @pl.when(t != 1)
+        @pl.when(t != 8)
         def _():
             messages(8, vg).wait_recv()
 
@@ -401,7 +401,7 @@
             for i in range(1, 8):
                 reply(8 * vg + (d + i) % 8, d).start()
 
-        @pl.when(t > 1)
+        @pl.when(jnp.logical_and(t > 0, t < 8))
         def _():
             for i in range(8):
                 reply(8 * vg + (d + i) % 8, d).start()
@@ -477,10 +477,11 @@
     spin_gain = time_step / (0.4 * mass * (3.0 * GRID / 16.0) ** 2)
     vel = [velocity_ref[m : m + 1, :] + force[m] * gain for m in range(3)]
     spin = [spin_ref[m : m + 1, :] + torque[m] * spin_gain for m in range(3)]
+    out_ref[...] = jnp.zeros_like(out_ref)
     for m in range(3):
-        new_velocity_ref[m : m + 1, :] = vel[m]
-        new_spin_ref[m : m + 1, :] = spin[m]
-        new_position_ref[m : m + 1, :] = pos[m] + time_step * vel[m]
+        out_ref[2, m : m + 1, :] = vel[m]
+        out_ref[3, m : m + 1, :] = spin[m]
+        out_ref[0, m : m + 1, :] = pos[m] + time_step * vel[m]
     vec = (x, y, z)
     turned = cross(spin, vec)
     quarter = 0.5 * time_step
@@ -488,7 +489,7 @@
     q += [vec[m] + quarter * (w * spin[m] + turned[m]) for m in range(3)]
     norm = jnp.sqrt(q[0] * q[0] + q[1] * q[1] + q[2] * q[2] + q[3] * q[3])
     for k in range(4):
-        new_quaternion_ref[k : k + 1, :] = q[k] / norm
+        out_ref[1, k : k + 1, :] = q[k] / norm
 
     messages(DEVS - 1, 0).wait_send()
     replies(DEVS - 1).wait_send()
@@ -498,27 +499,32 @@
 
 ROWS = 5
 SMALL = 12
-SCRATCH = 22
-
-
-def settle_kernel(*refs):
-    sem = refs[8]
-    copies = [pltpu.make_async_copy(refs[n], refs[4 + n], sem.at[n]) for n in range(4)]
+SCRATCH = 19
+
+
+OUT_ROWS = (3, 4, 3, 3)
+
+
+def settle_kernel(packed, *refs):
+    sem = refs[4]
+    copies = [
+        pltpu.make_async_copy(packed.at[n, pl.ds(0, rows)], refs[n], sem.at[n]) for n, rows in enumerate(OUT_ROWS)
+    ]
     for copy in copies:
         copy.start()
     for copy in copies:
         copy.wait()
 
 
-def settle(outs):
+def settle(packed):
     anywhere = pl.BlockSpec(memory_space=pl.ANY)
     return pl.pallas_call(
         settle_kernel,
-        out_shape=[jax.ShapeDtypeStruct(a.shape, a.dtype) for a in outs],
-        in_specs=[anywhere] * 4,
+        out_shape=[jax.ShapeDtypeStruct((rows, GRAINS), f32) for rows in OUT_ROWS],
+        in_specs=[anywhere],
         out_specs=[anywhere] * 4,
         scratch_shapes=[pltpu.SemaphoreType.DMA((4,))],
-    )(*outs)
+    )(packed)
 
 
 def body(
@@ -534,9 +540,9 @@
     )
     outs = pl.pallas_call(
         kernel,
-        out_shape=[jax.ShapeDtypeStruct((n, GRAINS), f32) for n in (3, 4, 3, 3)],
+        out_shape=jax.ShapeDtypeStruct((4, 4, GRAINS), f32),
         in_specs=[pl.BlockSpec(memory_space=pl.ANY)] * (1 + SMALL),
-        out_specs=[vmem] * 4,
+        out_specs=vmem,
         scratch_shapes=[
             pltpu.VMEM((GRAINS, SPAN, 32, GRID), bf16),
             pltpu.VMEM((128, 256), f32),

time: 40.7 us -> 40.7 us (level)
  no operation moved by 1% of the time
where the time goes in v5:
time: 40.7 us; the launch traced here: 40.6 us
  Pallas kernels  39.9 us (98%)
  between operations  0.64 us (2%)
    pallas_call x1, Pallas kernels, body(): pl.pallas_call(kernel, out_shape=jax.ShapeDtypeStruct((4, 4, GRAINS), f32...  38.6 us
    pallas_call x1, Pallas kernels, settle(): pl.pallas_call(settle_kernel, out_shape=[jax.ShapeDtypeStruct((rows, GRAI...  1.34 us

profile of v5, /device:TPU:24, one launch (start us, length us, event | category | flops | bytes accessed | tf_op | source)
XLA Modules:
  0.0 40.6 jit_solution(10492160291094364704)
XLA Ops:
  0.6 38.6 %shard_map.156.packed = f32[4,4,4]{2,1,0:T(4,128)} custom-call(bf16[4,64,64,64]{3,2,1,0:T(8,128)(2,1)} %level_ref.1, f32[3,4,512]{2,1,0:T(4,128)} %refs_0_.1, f32[3,4]{1,0:T(4,128)} %refs_1_.1, f32[4,4]{1,0:T(4,128)} %refs_2_.1, f32[3,4]{1,0:T(4,128)} %refs_3_.1, f32[3,4]{1,0:T(4,128)} %refs_4_.1, f32[1,4]{1,0:T(1,128)} %bitcast.5, s32[1,128]{1,0:T(1,128)} %bitcast.6, ...), custom_call_target="tpu_custom_call" | custom-call | tf_op jit(solution)/shard_map/pallas_call | solution.py:541
  39.2 1.3 %shard_map.157 = (f32[3,4]{1,0:T(4,128)}, f32[4,4]{1,0:T(4,128)}, f32[3,4]{1,0:T(4,128)}, f32[3,4]{1,0:T(4,128)}) custom-call(f32[4,4,4]{2,1,0:T(4,128)} %shard_map.156.packed), custom_call_target="tpu_custom_call" | custom-call | tf_op jit(solution)/shard_map/pallas_call | solution.py:521
